TPU v7x, 32 devices: a whole 2x2x4 slice. The times are simulated.
32 devices in a mesh: expert: 8 (over z, x), shard: 4 (over y, core).
Axes of the slice: x: 2, y: 2, z: 4, core: 2. Of those that a mesh axis runs over, the one named last changes fastest.
Arguments:
- hidden_in: bfloat16 [8192, 1536], P(('expert', 'shard')), may hold values from -6 to 6
- segment_ids: int32 [8192], P('expert'), may hold values from 0 to 4, as said below
- routes: int32 [8192, 4], P(('expert', 'shard')), may hold values from 0 to 7, all different within a row; in each aligned block of 256 rows (0 to 255, 256 to 511, ...) at most 256 rows name the same one
- attn_gain: bfloat16 [1536], P('shard'), may hold values from 0.099609375 to 1.8984375
- moe_gain: bfloat16 [1536], P('shard'), may hold values from 0.099609375 to 1.8984375
- w_query: bfloat16 [1536, 1536], P('shard'), may hold values from -0.15625 to 0.15625
- w_key: bfloat16 [1536, 256], P('shard'), may hold values from -0.15625 to 0.15625
- w_value: bfloat16 [1536, 256], P('shard'), may hold values from -0.15625 to 0.15625
- w_out: bfloat16 [1536, 1536], P('shard'), may hold values from -1.25 to 1.25
- w_router: bfloat16 [1536, 8], P('shard'), may hold values from -0.078125 to 0.078125
- expert_gate: bfloat16 [8, 1536, 768], P('expert'), may hold values from -0.15625 to 0.15625
- expert_up: bfloat16 [8, 1536, 768], P('expert'), may hold values from -0.15625 to 0.15625
- expert_down: bfloat16 [8, 768, 1536], P('expert'), may hold values from -0.4375 to 0.4375
- out_grad: bfloat16 [8192, 1536], P(('expert', 'shard')), may hold values from -6 to 6
Outputs:
- layer_out: bfloat16 [8192, 1536], P(('expert', 'shard'))
- input_grad: float32 [8192, 1536], P(('expert', 'shard'))
- attn_gain_grad: float32 [1536], P('shard')
- moe_gain_grad: float32 [1536], P('shard')
- w_query_grad: float32 [1536, 1536], P('shard')
- w_key_grad: float32 [1536, 256], P('shard')
- w_value_grad: float32 [1536, 256], P('shard')
- w_out_grad: float32 [1536, 1536], P('shard')
- w_router_grad: float32 [1536, 8], P('shard')
- expert_gate_grad: float32 [8, 1536, 768], P('expert')
- expert_up_grad: float32 [8, 1536, 768], P('expert')
- expert_down_grad: float32 [8, 768, 1536], P('expert')
Inputs may be any that keep to these rules, and one draw needn't show every extreme that they name: `segment_ids`: within each sequence of 1024 tokens the document numbers start at 0, never fall and step by one; every document has 64 tokens or more. `routes`: A token's 4 experts differ; among the tokens of one device no expert is named more than 256 times.
All inputs are finite; a program needn't handle non-finite values.
Results may differ from a plain program's by a relative error of at most 0.017.
Values may be sent and summed in bfloat16 or wider, within the bound.
No kernel may reach another device: no remote copies, remote signals or barrier semaphores. Data moves between devices by JAX's collectives and lax.ppermute only.
A program may use at most 192 MiB of HBM per device.

v0:
```python
import jax
import jax.numpy as jnp
from jax import lax
from jax.sharding import PartitionSpec as P

HQ = 12
KVH = 2
HEAD = 128


EPSILON = 1e-06
ROPE_BASE = 10000.0
MASKED_SCORE = -1e30
HIGHEST = lax.Precision.HIGHEST


def rope_tables(positions, head_size):
    half_size = head_size // 2
    frequency = ROPE_BASE ** (-(jnp.arange(half_size, dtype=jnp.float32) * 2.0 / head_size))
    angles = positions.astype(jnp.float32)[:, None] * frequency[None, :]
    return (jnp.cos(angles), jnp.sin(angles))


def rotate(values, cosine_table, sine_table, head_size):
    rows_count = values.shape[0]
    shaped = values.reshape(rows_count, -1, head_size)
    half_size = head_size // 2
    first_half = shaped[..., :half_size]
    second_half = shaped[..., half_size:]
    cosine_part = cosine_table[:, None, :]
    sine_part = sine_table[:, None, :]
    turned = jnp.concatenate(
        [
            first_half * cosine_part - second_half * sine_part,
            second_half * cosine_part + first_half * sine_part,
        ],
        -1,
    )
    return turned.reshape(rows_count, -1)


def norm_forward(values, gain):
    factor = lax.rsqrt(jnp.mean(values * values, -1, keepdims=True) + EPSILON)
    unit_rows = values * factor
    return (unit_rows, factor, (unit_rows * gain).astype(jnp.bfloat16))


def norm_backward(grad_rows, unit_rows, factor, gain):
    gain_grad = jnp.sum(grad_rows * unit_rows, 0)
    scaled_grad = grad_rows * gain
    return (
        factor * (scaled_grad - unit_rows * jnp.mean(scaled_grad * unit_rows, -1, keepdims=True)),
        gain_grad,
    )


def score_block(query_heads, key_heads, visible, score_scale):
    raw_scores = jnp.einsum(
        "tkgd,skd->kgts", query_heads, key_heads, preferred_element_type=jnp.float32
    )
    return jnp.where(visible, raw_scores * score_scale, MASKED_SCORE)


def on_device(
    hidden_in,
    segment_ids,
    routes,
    attn_gain,
    moe_gain,
    w_query,
    w_key,
    w_value,
    w_out,
    w_router,
    expert_gate,
    expert_up,
    expert_down,
    out_grad,
):
    tok_rows = hidden_in.shape[0]
    top_count = routes.shape[1]
    experts = w_router.shape[1]
    capacity = tok_rows * top_count * 2 // experts
    groups = HQ // KVH
    score_scale = HEAD ** (-0.5)
    shard_index = lax.axis_index("shard")
    n_expert = lax.axis_size("expert")
    local_experts = expert_gate.shape[0]
    gain_attn, gain_moe, query_w, key_w, value_w, out_w, router_w = (
        lax.all_gather(attn_gain, "shard", axis=0, tiled=True),
        lax.all_gather(moe_gain, "shard", axis=0, tiled=True),
        lax.all_gather(w_query, "shard", axis=0, tiled=True),
        lax.all_gather(w_key, "shard", axis=0, tiled=True),
        lax.all_gather(w_value, "shard", axis=0, tiled=True),
        lax.all_gather(w_out, "shard", axis=0, tiled=True),
        lax.all_gather(w_router, "shard", axis=0, tiled=True),
    )
    gain_attn = gain_attn.astype(jnp.float32)
    gain_moe = gain_moe.astype(jnp.float32)
    inputs = hidden_in.astype(jnp.float32)
    unit_attn, factor_attn, normed = norm_forward(inputs, gain_attn)
    q_pre = jnp.dot(normed, query_w, preferred_element_type=jnp.float32)
    k_pre = jnp.dot(normed, key_w, preferred_element_type=jnp.float32)
    value_rows = jnp.dot(normed, value_w, preferred_element_type=jnp.float32).astype(jnp.bfloat16)
    positions = shard_index * tok_rows + jnp.arange(tok_rows, dtype=jnp.int32)
    cosine_table, sine_table = rope_tables(positions, HEAD)
    queries = rotate(q_pre, cosine_table, sine_table, HEAD).astype(jnp.bfloat16)
    key_local = rotate(k_pre, cosine_table, sine_table, HEAD).astype(jnp.bfloat16)
    key_rows, value_all = (
        lax.all_gather(key_local, "shard", axis=0, tiled=True),
        lax.all_gather(value_rows, "shard", axis=0, tiled=True),
    )
    seq_len = key_rows.shape[0]
    query_heads = queries.reshape(tok_rows, KVH, groups, HEAD)
    key_heads = key_rows.reshape(seq_len, KVH, HEAD)
    value_heads = value_all.reshape(seq_len, KVH, HEAD)
    seg_local = lax.dynamic_slice_in_dim(segment_ids, shard_index * tok_rows, tok_rows)
    visible = (positions[:, None] >= jnp.arange(seq_len, dtype=jnp.int32)[None, :]) & (
        seg_local[:, None] == segment_ids[None, :]
    )
    score_values = score_block(query_heads, key_heads, visible, score_scale)
    top_score = jnp.max(score_values, -1, keepdims=True)
    exponent = jnp.exp(score_values - top_score)
    denominators = jnp.sum(exponent, -1, keepdims=True)
    probabilities = exponent / denominators
    log_total = top_score + jnp.log(denominators)
    attended = (
        jnp.einsum(
            "kgts,skd->tkgd",
            probabilities.astype(jnp.bfloat16),
            value_heads,
            preferred_element_type=jnp.float32,
        )
        .reshape(tok_rows, -1)
        .astype(jnp.bfloat16)
    )
    mid_state = inputs + jnp.dot(attended, out_w, preferred_element_type=jnp.float32)
    unit_moe, factor_moe, normed_moe = norm_forward(mid_state, gain_moe)
    logits = jnp.dot(normed_moe, router_w, preferred_element_type=jnp.float32)
    onehot = (routes[:, :, None] == jnp.arange(experts, dtype=jnp.int32)[None, None, :]).astype(
        jnp.float32
    )
    chosen = jnp.sum(onehot * logits[:, None, :], -1)
    chosen = chosen - jnp.max(chosen, -1, keepdims=True)
    weights = jnp.exp(chosen)
    gate = weights / jnp.sum(weights, -1, keepdims=True)
    flat_routes = routes.reshape(-1)
    route_hot = (flat_routes[:, None] == jnp.arange(experts, dtype=jnp.int32)[None, :]).astype(
        jnp.int32
    )
    before = jnp.cumsum(route_hot, 0, dtype=jnp.int32) - route_hot
    slot_id = flat_routes * capacity + jnp.sum(before * route_hot, 1, dtype=jnp.int32)
    source = (
        jnp.zeros((experts * capacity,), jnp.int32)
        .at[slot_id]
        .set(jnp.arange(tok_rows * top_count, dtype=jnp.int32))
    )
    filled = jnp.zeros((experts * capacity,), jnp.bool_).at[slot_id].set(True)
    outgoing = jnp.where(filled[:, None], jnp.take(normed_moe, source // top_count, axis=0), 0)
    outgoing = outgoing.reshape(experts, capacity, -1)
    arrived = lax.all_to_all(outgoing, "expert", split_axis=0, concat_axis=0, tiled=True)
    item_count = arrived.shape[1]
    shaped = arrived.reshape(n_expert, local_experts, item_count, -1)
    gate_pre = jnp.einsum("nlcd,ldf->nlcf", shaped, expert_gate, preferred_element_type=jnp.float32)
    up_pre = jnp.einsum("nlcd,ldf->nlcf", shaped, expert_up, preferred_element_type=jnp.float32)
    hidden_rows = (gate_pre * jax.nn.sigmoid(gate_pre) * up_pre).astype(jnp.bfloat16)
    result = jnp.einsum(
        "nlcf,lfd->nlcd", hidden_rows, expert_down, preferred_element_type=jnp.float32
    )
    result = result.astype(jnp.bfloat16).reshape(arrived.shape)
    returned = lax.all_to_all(result, "expert", split_axis=0, concat_axis=0, tiled=True)
    outcome = (
        returned,
        arrived,
        gate_pre.reshape(n_expert * local_experts, item_count, -1),
        up_pre.reshape(n_expert * local_experts, item_count, -1),
        hidden_rows.reshape(n_expert * local_experts, item_count, -1),
    )
    returned_rows = jnp.take(outcome[0].reshape(experts * capacity, -1), slot_id, axis=0).reshape(
        tok_rows, top_count, -1
    )
    mixed = mid_state + jnp.sum(gate[:, :, None] * returned_rows, 1)
    layer_out = mixed.astype(jnp.bfloat16)
    grad_out = out_grad.astype(jnp.float32)
    gate_grad = jnp.sum(returned_rows * grad_out[:, None, :], -1)
    gate_slots = jnp.take(gate.reshape(-1), source, axis=0)
    d_send = jnp.where(
        filled[:, None], jnp.take(grad_out, source // top_count, axis=0) * gate_slots[:, None], 0.0
    )
    d_send = d_send.astype(jnp.bfloat16).reshape(experts, capacity, -1)
    d_arrived = lax.all_to_all(d_send, "expert", split_axis=0, concat_axis=0, tiled=True)
    d_shaped = d_arrived.reshape(n_expert, local_experts, capacity, -1)
    arrived_rows = outcome[1].reshape(n_expert, local_experts, capacity, -1)
    gate_pre = outcome[2].reshape(n_expert, local_experts, capacity, -1)
    up_pre = outcome[3].reshape(n_expert, local_experts, capacity, -1)
    hidden_rows = outcome[4].reshape(n_expert, local_experts, capacity, -1)
    sigmoid_gate = jax.nn.sigmoid(gate_pre)
    d_hidden = jnp.einsum(
        "nlcd,lfd->nlcf", d_shaped, expert_down, preferred_element_type=jnp.float32
    )
    down_grad = jnp.einsum(
        "nlcf,nlcd->lfd", hidden_rows, d_shaped, preferred_element_type=jnp.float32
    )
    d_gate = (d_hidden * up_pre * sigmoid_gate * (1.0 + gate_pre * (1.0 - sigmoid_gate))).astype(
        jnp.bfloat16
    )
    d_up = (d_hidden * gate_pre * sigmoid_gate).astype(jnp.bfloat16)
    gate_w_grad = jnp.einsum(
        "nlcd,nlcf->ldf", arrived_rows, d_gate, preferred_element_type=jnp.float32
    )
    up_w_grad = jnp.einsum("nlcd,nlcf->ldf", arrived_rows, d_up, preferred_element_type=jnp.float32)
    d_rows = jnp.einsum("nlcf,ldf->nlcd", d_gate, expert_gate, preferred_element_type=jnp.float32)
    d_rows = d_rows + jnp.einsum(
        "nlcf,ldf->nlcd", d_up, expert_up, preferred_element_type=jnp.float32
    )
    d_rows = d_rows.astype(jnp.bfloat16).reshape(experts, capacity, -1)
    d_returned = lax.all_to_all(d_rows, "expert", split_axis=0, concat_axis=0, tiled=True)
    expert_sums = (
        lax.psum(gate_w_grad.astype(jnp.bfloat16), "shard").astype(jnp.float32),
        lax.psum(up_w_grad.astype(jnp.bfloat16), "shard").astype(jnp.float32),
        lax.psum(down_grad.astype(jnp.bfloat16), "shard").astype(jnp.float32),
    )
    d_copies = jnp.take(d_returned.reshape(experts * capacity, -1), slot_id, axis=0).reshape(
        tok_rows, top_count, -1
    )
    d_normed_moe = jnp.sum(d_copies, 1, dtype=jnp.float32)
    d_chosen = gate * (gate_grad - jnp.sum(gate * gate_grad, -1, keepdims=True))
    d_logits = jnp.sum(onehot * d_chosen[:, :, None], 1)
    router_f32 = router_w.astype(jnp.float32)
    d_normed_moe = d_normed_moe + jnp.dot(d_logits, router_f32.T, precision=HIGHEST)
    router_grad = jnp.dot(normed_moe.astype(jnp.float32).T, d_logits, precision=HIGHEST)
    d_mid_norm, gain_moe_grad = norm_backward(d_normed_moe, unit_moe, factor_moe, gain_moe)
    d_mid = grad_out + d_mid_norm
    d_branch = d_mid.astype(jnp.bfloat16)
    out_w_grad = jnp.dot(attended.T, d_branch, preferred_element_type=jnp.float32)
    d_attended = jnp.dot(d_branch, out_w.T, preferred_element_type=jnp.float32).astype(jnp.bfloat16)
    d_attended = d_attended.reshape(tok_rows, KVH, groups, HEAD)
    score_again = score_block(query_heads, key_heads, visible, score_scale)
    prob_again = jnp.exp(score_again - log_total)
    d_probs = jnp.einsum(
        "tkgd,skd->kgts", d_attended, value_heads, preferred_element_type=jnp.float32
    )
    d_scores = (
        prob_again * (d_probs - jnp.sum(prob_again * d_probs, -1, keepdims=True)) * score_scale
    )
    d_scores = d_scores.astype(jnp.bfloat16)
    d_query = jnp.einsum(
        "kgts,skd->tkgd", d_scores, key_heads, preferred_element_type=jnp.float32
    ).reshape(tok_rows, -1)
    d_key_part = jnp.einsum(
        "kgts,tkgd->skd", d_scores, query_heads, preferred_element_type=jnp.float32
    ).reshape(seq_len, -1)
    d_value_part = jnp.einsum(
        "kgts,tkgd->skd",
        prob_again.astype(jnp.bfloat16),
        d_attended,
        preferred_element_type=jnp.float32,
    ).reshape(seq_len, -1)
    d_keys, d_values = (
        lax.psum_scatter(
            d_key_part.astype(jnp.bfloat16), "shard", scatter_dimension=0, tiled=True
        ).astype(jnp.float32),
        lax.psum_scatter(
            d_value_part.astype(jnp.bfloat16), "shard", scatter_dimension=0, tiled=True
        ).astype(jnp.float32),
    )
    d_q_pre = rotate(d_query, cosine_table, -sine_table, HEAD).astype(jnp.bfloat16)
    d_k_pre = rotate(d_keys, cosine_table, -sine_table, HEAD).astype(jnp.bfloat16)
    d_v_pre = d_values.astype(jnp.bfloat16)
    query_grad = jnp.dot(normed.T, d_q_pre, preferred_element_type=jnp.float32)
    key_grad = jnp.dot(normed.T, d_k_pre, preferred_element_type=jnp.float32)
    value_grad = jnp.dot(normed.T, d_v_pre, preferred_element_type=jnp.float32)
    d_normed = jnp.dot(d_q_pre, query_w.T, preferred_element_type=jnp.float32)
    d_normed = d_normed + jnp.dot(d_k_pre, key_w.T, preferred_element_type=jnp.float32)
    d_normed = d_normed + jnp.dot(d_v_pre, value_w.T, preferred_element_type=jnp.float32)
    d_input_norm, gain_attn_grad = norm_backward(d_normed, unit_attn, factor_attn, gain_attn)
    input_grad = d_mid + d_input_norm
    partial_sums = (
        gain_attn_grad,
        gain_moe_grad,
        query_grad,
        key_grad,
        value_grad,
        out_w_grad,
        router_grad,
    )
    summed = lax.psum(
        (
            partial_sums[0],
            partial_sums[1],
            partial_sums[2],
            partial_sums[3],
            partial_sums[4],
            partial_sums[5],
            partial_sums[6],
        ),
        ("expert", "shard"),
    )
    n_shard = lax.axis_size("shard")
    owned_grads = tuple(
        (
            lax.dynamic_slice_in_dim(
                member, shard_index * (member.shape[0] // n_shard), member.shape[0] // n_shard, 0
            )
            for member in summed
        )
    )
    return (
        layer_out,
        input_grad,
        owned_grads[0],
        owned_grads[1],
        owned_grads[2],
        owned_grads[3],
        owned_grads[4],
        owned_grads[5],
        owned_grads[6],
        expert_sums[0],
        expert_sums[1],
        expert_sums[2],
    )


def solution(mesh):
    placed = (
        P(("expert", "shard"), None),
        P("expert"),
        P(("expert", "shard"), None),
        P("shard"),
        P("shard"),
        P("shard", None),
        P("shard", None),
        P("shard", None),
        P("shard", None),
        P("shard", None),
        P("expert", None, None),
        P("expert", None, None),
        P("expert", None, None),
        P(("expert", "shard"), None),
    )
    return jax.shard_map(
        on_device,
        mesh=mesh,
        in_specs=placed,
        out_specs=(
            P(("expert", "shard"), None),
            P(("expert", "shard"), None),
            P("shard"),
            P("shard"),
            P("shard", None),
            P("shard", None),
            P("shard", None),
            P("shard", None),
            P("shard", None),
            P("expert", None, None),
            P("expert", None, None),
            P("expert", None, None),
        ),
        check_vma=False,
    )
```

profile of v0, /device:TPU:0, one launch (start us, length us, event | category | flops | bytes accessed | tf_op | source)
XLA Modules:
  0.0 1429.1 jit_solution(12877226158871589504)
XLA Ops:
  18.5 13.6 all_gather.28
  34.5 11.1 all_gather.29
  67.8 13.5 all_gather.30
  82.7 11.4 all_gather.31
  117.9 10.1 gather_fusion
  132.3 144.5 %all_to_all.20 = bf16[8,256,1536]{2,1,0:T(8,128)(2,1)S(1)} all-to-all(bf16[8,256,1536]{2,1,0:T(8,128)(2,1)S(1)} %select_select_fusion), channel_id=1, replica_groups=mesh['expert'=8,'shard'=4] {'expert'}, dimensions={0} | all-to-all | bytes 12582912 | tf_op jit(solution)/shard_map/all_to_all | solution.py:161
  282.0 7.4 fusion.13
  309.7 7.7 mul.406
  317.5 15.8 %gather_fusion.1 = f32[2048,1536]{1,0:T(8,128)} fusion(f32[256,1536]{1,0:T(8,128)} %convert_element_type.193, s32[2048]{0:T(1024)S(1)} %copy-done.42), kind=kCustom, calls=%fused_computation.3 | custom fusion | bytes 25174016 | tf_op jit(solution)/shard_map/jit(_take)/gather | solution.py:188
  339.1 101.4 %all-to-all-done.1 = bf16[8,256,1536]{2,1,0:T(8,128)(2,1)} async-done(((bf16[8,256,1536]{2,1,0:T(8,128)(2,1)}), bf16[8,256,1536]{2,1,0:T(8,128)(2,1)}, u32[]{:S(2)}, u32[]{:S(2)}) %all-to-all-start.1) | async-done | bytes 6291488 | tf_op jit(solution)/shard_map/all_to_all | solution.py:171
  440.5 10.9 gather_fusion.3
  456.6 8.6 gather_fusion.2
  471.3 141.7 %all_to_all.21 = bf16[8,256,1536]{2,1,0:T(8,128)(2,1)S(1)} all-to-all(bf16[8,256,1536]{2,1,0:T(8,128)(2,1)S(1)} %select_convert_fusion), channel_id=1, replica_groups=mesh['expert'=8,'shard'=4] {'expert'}, dimensions={0} | all-to-all | bytes 12582912 | tf_op jit(solution)/shard_map/all_to_all | solution.py:191
  613.0 11.7 fusion.12
  624.7 8.3 fusion.24
  633.0 10.4 add_convert_fusion
  648.9 9.3 fusion.34
  658.2 127.3 %all-to-all-done.3 = bf16[8,256,1536]{2,1,0:T(8,128)(2,1)} async-done(((bf16[8,256,1536]{2,1,0:T(8,128)(2,1)}), bf16[8,256,1536]{2,1,0:T(8,128)(2,1)}, u32[]{:S(2)}, u32[]{:S(2)}) %all-to-all-start.3) | async-done | bytes 6291488 | tf_op jit(solution)/shard_map/all_to_all | solution.py:217
  785.5 10.9 gather_fusion.4
  796.3 8.3 select_convert_fusion.1
  804.6 7.6 reshape.455
  812.2 8.5 multiply_reduce_fusion.1
  820.7 7.8 reshape.456
  828.6 7.8 reduce_sum.156
  851.3 18.9 %fusion.68 = bf16[2,128,1024]{2,1,0:T(8,128)(2,1)} fusion(bf16[256,2,6,128]{0,3,2,1:T(8,128)(2,1)S(1)} %bitcast.294, f32[2,1024,256,6]{2,1,3,0:T(8,128)} %fusion.71, f32[2,6,256]{2,1,0:T(8,128)S(1)} %log_add_fusion, f32[2,1024,256,6]{2,1,3,0:T(8,128)} %copy-done.4, pred[256,1024]{0,1:T(8,128)(4,1)S(1)} %copy-done.17), kind=kOutput, calls=%fused_computation.100 | convolution fusion | flops 840175616 | bytes 26750976 | tf_op jit(solution)/shard_map/kgts,tkgd->skd/dot_general | solution.py:250
  870.3 9.4 fusion.28
  879.7 8.7 fusion.65
  888.5 9.3 fusion.31
  898.8 21.0 %fusion.39 = f32[2,128,6,256]{3,1,2,0:T(8,128)} fusion(bf16[1024,2,128,1]{0,2,3,1:T(8,128)(2,1)S(1)} %bitcast.298, f32[2,1024,256,6]{2,1,3,0:T(8,128)} %fusion.71, f32[2,6,256]{2,1,0:T(8,128)S(1)} %log_add_fusion, f32[2,1024,256,6]{2,1,3,0:T(8,128)} %copy-done.4, pred[256,1024]{0,1:T(8,128)(4,1)S(1)} %copy-done.17), kind=kOutput, calls=%fused_computation.67 | convolution fusion | flops 839913472 | bytes 27537408 | tf_op jit(solution)/shard_map/kgts,skd->tkgd/dot_general | solution.py:247
  939.5 112.2 %all-reduce.8.cloned.1.call-done = (bf16[1,1536,768]{2,1,0:T(8,128)(2,1)}, bf16[1,1536,768]{2,1,0:T(8,128)(2,1)}, bf16[1,768,1536]{2,1,0:T(8,128)(2,1)}) async-done(((bf16[1,1536,768]{2,1,0:T(8,128)(2,1)}, bf16[1,1536,768]{2,1,0:T(8,128)(2,1)}, bf16[1,768,1536]{2,1,0:T(8,128)(2,1)}), (bf16[1,1536,768]{2,1,0:T(8,128)(2,1)}, bf16[1,1536,768]{2,1,0:T(8,128)(2,1)}, ...) | async-done | bytes 7077904 | tf_op jit(solution)/shard_map/psum | solution.py:219
  1065.3 42.1 %all-reduce = (f32[1536]{0:T(1024)S(1)}, f32[1536]{0:T(1024)S(1)}, f32[1536,8]{0,1:T(8,128)S(1)}) all-reduce(f32[1536]{0:T(1024)S(1)} %get-tuple-element.15, f32[1536]{0:T(1024)S(1)} %get-tuple-element.13, f32[1536,8]{0,1:T(8,128)S(1)} %fusion.119), channel_id=1, replica_groups=mesh['expert'=8,'shard'=4] {'expert','shard'}, use_global_device_ids=true, to_apply=%region_23.25 | all-reduce | flops 15360 | bytes 122880 | tf_op jit(solution)/shard_map/psum | solution.py:287
  1112.4 302.4 %all-reduce.6.cloned.1.call-done = (f32[1536,1536]{1,0:T(8,128)}, f32[1536,256]{1,0:T(8,128)}, f32[1536,256]{1,0:T(8,128)}, f32[1536,1536]{1,0:T(8,128)}) async-done(((f32[1536,1536]{1,0:T(8,128)}, f32[1536,256]{1,0:T(8,128)}, f32[1536,256]{1,0:T(8,128)}, f32[1536,1536]{1,0:T(8,128)}), (f32[1536,1536]{1,0:T(8,128)}, f32[1536,256]{1,0:T(8,128)}, f32[1536,256]{1,0:T(8,128)}, ...) | async-done | bytes 22020112 | tf_op jit(solution)/shard_map/psum | solution.py:287
  (266 shorter events, 173.9 us)
Async XLA Ops:
  7.2 283.9 %copy-start = (bf16[1,768,1536]{2,1,0:T(8,128)(2,1)S(1)}, bf16[1,768,1536]{2,1,0:T(8,128)(2,1)}, u32[]{:S(2)}) copy-start(bf16[1,768,1536]{2,1,0:T(8,128)(2,1)} %param.28) | copy-start | bytes 7077892
  7.2 38.4 %copy-start.58 = (bf16[384]{0:T(512)(128)(2,1)S(1)}, bf16[384]{0:T(512)(128)(2,1)}, u32[]{:S(2)}) copy-start(bf16[384]{0:T(512)(128)(2,1)} %param.20) | copy-start | bytes 2308
  7.2 89.2 %all-gather.5.cloned.1.call-start = ((), (), s32[]{:S(2)}) async-start(), calls=%async_computation.6 | async-start | bytes 5898240 | tf_op jit(solution)/shard_map/all_gather | solution.py:92
  7.9 73.4 %copy-start.5 = (bf16[256,1536]{1,0:T(8,128)(2,1)S(1)}, bf16[256,1536]{1,0:T(8,128)(2,1)}, u32[]{:S(2)}) copy-start(bf16[256,1536]{1,0:T(8,128)(2,1)} %param.16) | copy-start | bytes 2359300
  8.0 104.5 %all-gather.7.cloned.1.call-start = ((), (), s32[]{:S(2)}) async-start(), calls=%async_computation.7 | async-start | bytes 5898240 | tf_op jit(solution)/shard_map/all_gather | solution.py:95
  17.0 79.4 %copy-start.34 = (f32[1536]{0:T(1024)}, f32[1536]{0:T(1024)S(1)}, u32[]{:S(2)}) copy-start(f32[1536]{0:T(1024)S(1)} %reshape.524) | copy-start | bytes 18436
  18.5 48.4 %copy-start.50 = (f32[256]{0:T(256)}, f32[256]{0:T(256)S(1)}, u32[]{:S(2)}) copy-start(f32[256]{0:T(256)S(1)} %add_rsqrt_fusion.1) | copy-start | bytes 3076
  53.9 13.9 copy-start.45
  55.8 60.7 %copy-start.38 = (f32[1536]{0:T(1024)}, f32[1536]{0:T(1024)S(1)}, u32[]{:S(2)}) copy-start(f32[1536]{0:T(1024)S(1)} %reshape.525) | copy-start | bytes 18436
  56.1 11.7 copy-start.47
  67.8 33.0 %copy-start.30 = (f32[256,64]{0,1:T(8,128)}, f32[256,64]{0,1:T(8,128)S(1)}, u32[]{:S(2)}) copy-start(f32[256,64]{0,1:T(8,128)S(1)} %get-tuple-element.45) | copy-start | bytes 196612
  81.4 12.7 copy-start.22
  116.6 11.5 copy-start.55
  117.9 220.8 %copy-start.2 = (bf16[256,1536]{1,0:T(8,128)(2,1)}, bf16[256,1536]{1,0:T(8,128)(2,1)S(1)}, u32[]{:S(2)}) copy-start(bf16[256,1536]{1,0:T(8,128)(2,1)S(1)} %multiply_convert_fusion) | copy-start | bytes 2359300
  132.3 144.5 %copy-start.59 = (bf16[1,1536,768]{2,1,0:T(8,128)(2,1)S(1)}, bf16[1,1536,768]{2,1,0:T(8,128)(2,1)}, u32[]{:S(2)}) copy-start(bf16[1,1536,768]{2,1,0:T(8,128)(2,1)} %param.26) | copy-start | bytes 7077892
  298.0 142.5 %all-to-all-start.1 = ((bf16[8,256,1536]{2,1,0:T(8,128)(2,1)}), bf16[8,256,1536]{2,1,0:T(8,128)(2,1)}, u32[]{:S(2)}, u32[]{:S(2)}) async-start(bf16[8,256,1536]{2,1,0:T(8,128)(2,1)} %convolution_convert_fusion), calls=%async_computation.1 | async-start | bytes 12582912 | tf_op jit(solution)/shard_map/all_to_all | solution.py:171
  317.5 15.8 %copy-start.57 = (bf16[384,8]{0,1:T(8,128)(2,1)S(1)}, bf16[384,8]{0,1:T(8,128)(2,1)}, u32[]{:S(2)}) copy-start(bf16[384,8]{0,1:T(8,128)(2,1)} %param.25) | copy-start | bytes 18436
  317.5 21.2 %copy-start.46 = (s32[1024]{0:T(1024)S(1)}, s32[1024]{0:T(1024)}, u32[]{:S(2)}) copy-start(s32[1024]{0:T(1024)} %copy-done.45) | copy-start | bytes 12292
  317.5 21.2 %copy-start.48 = (s32[1024]{0:T(1024)S(1)}, s32[1024]{0:T(1024)}, u32[]{:S(2)}) copy-start(s32[1024]{0:T(1024)} %copy-done.47) | copy-start | bytes 12292
  317.5 21.5 %copy-start.49 = (s32[256,4]{0,1:T(4,128)S(1)}, s32[256,4]{0,1:T(4,128)}, u32[]{:S(2)}) copy-start(s32[256,4]{0,1:T(4,128)} %param.18) | copy-start | bytes 12292
  613.0 11.7 copy-start.15
  613.0 11.7 copy-start.60
  643.4 142.0 %all-to-all-start.3 = ((bf16[8,256,1536]{2,1,0:T(8,128)(2,1)}), bf16[8,256,1536]{2,1,0:T(8,128)(2,1)}, u32[]{:S(2)}, u32[]{:S(2)}) async-start(bf16[8,256,1536]{2,1,0:T(8,128)(2,1)} %add_convert_fusion), calls=%async_computation.3 | async-start | bytes 12582912 | tf_op jit(solution)/shard_map/all_to_all | solution.py:217
  648.3 284.3 %reduce-scatter.3.cloned.1.call-start = ((), (), s32[]{:S(2)}) async-start(), calls=%async_computation.8 | async-start | bytes 655360 | tf_op jit(solution)/shard_map/reduce_scatter | solution.py:260
  870.2 65.1 %reduce-scatter.5.cloned.1.call-start = ((), (), s32[]{:S(2)}) async-start(), calls=%async_computation.9 | async-start | bytes 655360 | tf_op jit(solution)/shard_map/reduce_scatter | solution.py:263
  888.5 163.3 %all-reduce.8.cloned.1.call-start = ((), (), s32[]{:S(2)}) async-start(), calls=%async_computation.11 | async-start | bytes 14155776 | tf_op jit(solution)/shard_map/psum | solution.py:219
  897.8 22.0 %copy-start.31 = (f32[256,64]{0,1:T(8,128)S(1)}, f32[256,64]{0,1:T(8,128)}, u32[]{:S(2)}) copy-start(f32[256,64]{0,1:T(8,128)} %copy-done.30) | copy-start | bytes 196612
  897.8 22.0 %copy-start.32 = (f32[256,64]{0,1:T(8,128)S(1)}, f32[256,64]{0,1:T(8,128)}, u32[]{:S(2)}) copy-start(f32[256,64]{0,1:T(8,128)} %get-tuple-element.43) | copy-start | bytes 196612
  897.8 23.7 %copy-start.35 = (f32[1536]{0:T(1024)S(1)}, f32[1536]{0:T(1024)}, u32[]{:S(2)}) copy-start(f32[1536]{0:T(1024)} %copy-done.34) | copy-start | bytes 18436
  897.9 23.7 %copy-start.51 = (f32[256]{0:T(256)S(1)}, f32[256]{0:T(256)}, u32[]{:S(2)}) copy-start(f32[256]{0:T(256)} %copy-done.50) | copy-start | bytes 3076
  897.9 516.9 %all-reduce.6.cloned.1.call-start = ((), (), s32[]{:S(2)}) async-start(), calls=%async_computation.10 | async-start | bytes 44040192 | tf_op jit(solution)/shard_map/psum | solution.py:287
  1063.0 46.4 %copy-start.11 = (f32[256,1536]{1,0:T(8,128)S(1)}, f32[256,1536]{1,0:T(8,128)}, u32[]{:S(2)}) copy-start(f32[256,1536]{1,0:T(8,128)} %copy-done.9) | copy-start | bytes 4718596
  (47 other events, 250.6 us)
Sparse Core Ops, SparseCore 0:
  9.6 47.0 all-gather.4
  58.3 44.6 all-gather.6
  870.4 20.8 reduce-scatter.2
  894.3 21.6 reduce-scatter.4
  919.0 132.7 all-reduce.7
  1058.0 356.6 all-reduce.5
where the time goes:
time: 1440 us; the launch traced here: 1430 us
  waiting for transfers between devices  645 us (45%)
  blocking collectives  395 us (27%)
  matrix products  175 us (12%)
  local copies, waits for them, and re-layouts  118 us (8%)
  other arithmetic  71.5 us (5%)
  between operations  15.6 us (1%)
    psum x1, waiting for transfers between devices, on_device(): lax.psum((partial_sums[0], partial_sums[1], partial_sums[2], partial_sums...  302 us
    all_to_all x1, blocking collectives, on_device(): lax.all_to_all(outgoing, 'expert', split_axis=0, concat_axis=0, tiled=True)  144 us
    all_to_all x1, blocking collectives, on_device(): lax.all_to_all(d_send, 'expert', split_axis=0, concat_axis=0, tiled=True)  142 us
    all_to_all x1, waiting for transfers between devices, on_device(): lax.all_to_all(d_rows, 'expert', split_axis=0, concat_axis=0, tiled=True)  127 us
    psum x1, waiting for transfers between devices, on_device(): lax.psum(gate_w_grad.astype(jnp.bfloat16), 'shard').astype(jnp.float32)  112 us
    all_to_all x1, waiting for transfers between devices, on_device(): lax.all_to_all(result, 'expert', split_axis=0, concat_axis=0, tiled=True)  101 us
    psum x1, blocking collectives, on_device(): lax.psum((partial_sums[0], partial_sums[1], partial_sums[2], partial_sums...  42.1 us
  transfers between devices with their start and end apart: 8, of which 4 were waited for; matrix products, arithmetic and copies ran while one was open for 12% of the time, Pallas kernels for 0%

commit v1 on v0

--- a/solution.py
+++ b/solution.py
@@ -1,6 +1,10 @@
+import functools
+
 import jax
 import jax.numpy as jnp
 from jax import lax
+from jax.experimental import pallas as pl
+from jax.experimental.pallas import tpu as pltpu
 from jax.sharding import PartitionSpec as P
 
 HQ = 12
@@ -61,7 +65,7 @@
     return jnp.where(visible, raw_scores * score_scale, MASKED_SCORE)
 
 
-def on_device(
+def on_device_routed(
     hidden_in,
     segment_ids,
     routes,
@@ -321,6 +325,624 @@
     )
 
 
+AXES = ("expert", "shard")
+N_EXPERT = 8
+N_SHARD = 4
+LANES = 128
+MEBIBYTE = 1 << 20
+BF16 = jnp.bfloat16
+F32 = jnp.float32
+
+
+def swap(values, expert_bits, shard_bits):
+    pairs = [
+        (e * N_SHARD + s, (e ^ expert_bits) * N_SHARD + (s ^ shard_bits))
+        for e in range(N_EXPERT)
+        for s in range(N_SHARD)
+    ]
+    return lax.ppermute(values, AXES, pairs)
+
+
+def next_plane(values):
+    pairs = [
+        (e * N_SHARD + s, ((e + 2) % N_EXPERT) * N_SHARD + s)
+        for e in range(N_EXPERT)
+        for s in range(N_SHARD)
+    ]
+    return lax.ppermute(values, AXES, pairs)
+
+
+def gather_shards(values):
+    other_core = swap(values, 0, 1)
+    other_y = swap(values, 0, 2)
+    return [values, other_core, other_y, swap(other_y, 0, 1)]
+
+
+def xor_blocks(blocks, index):
+    odd = (index & 1) == 1
+    high = (index & 2) == 2
+    once = [jnp.where(odd, blocks[j ^ 1], blocks[j]) for j in range(4)]
+    return [jnp.where(high, once[j ^ 2], once[j]) for j in range(4)]
+
+
+def rejoin(mine, partner, low_first):
+    return jnp.where(
+        low_first,
+        jnp.concatenate([mine, partner], 0),
+        jnp.concatenate([partner, mine], 0),
+    )
+
+
+def dot_nn(left, right):
+    return lax.dot_general(left, right, (((1,), (0,)), ((), ())), preferred_element_type=F32)
+
+
+def dot_nt(left, right):
+    return lax.dot_general(left, right, (((1,), (1,)), ((), ())), preferred_element_type=F32)
+
+
+def dot_tn(left, right):
+    return lax.dot_general(left, right, (((0,), (0,)), ((), ())), preferred_element_type=F32)
+
+
+def turn(values, cosine, sine):
+    return values * cosine + pltpu.roll(values, HEAD // 2, 1) * sine
+
+
+def attention_forward_body(
+    where_ref, h1_ref, w0, w1, w2, w3, key_ref, value_ref, cos_ref, sin_ref, segq_ref, segk_ref,
+    query_out, prob_out, attended_out, bias_ref,
+):
+    rows, seq_len = bias_ref.shape
+
+    @pl.when(pl.program_id(0) == 0)
+    def _():
+        base = where_ref[0] * rows
+        query_pos = base + lax.broadcasted_iota(jnp.int32, (rows, seq_len), 0)
+        key_pos = lax.broadcasted_iota(jnp.int32, (rows, seq_len), 1)
+        visible = (query_pos >= key_pos) & (segq_ref[...] == segk_ref[...])
+        bias_ref[...] = jnp.where(visible, 0.0, MASKED_SCORE)
+
+    depth = w0.shape[0]
+    pre = dot_nn(h1_ref[:, :depth], w0[...])
+    for j, weight in enumerate((w1, w2, w3)):
+        pre = pre + dot_nn(h1_ref[:, (j + 1) * depth : (j + 2) * depth], weight[...])
+    for h in range(pre.shape[1] // HEAD):
+        cols = slice(h * HEAD, (h + 1) * HEAD)
+        query = turn(pre[:, cols], cos_ref[...], sin_ref[...]).astype(BF16)
+        query_out[:, cols] = query
+        scores = dot_nt(query, key_ref[...]) * HEAD ** (-0.5) + bias_ref[...]
+        exponent = jnp.exp(scores - jnp.max(scores, -1, keepdims=True))
+        total = jnp.sum(exponent, -1, keepdims=True)
+        probs = (exponent * (1.0 / total)).astype(BF16)
+        prob_out[h] = probs
+        attended_out[:, cols] = dot_nn(probs, value_ref[...]).astype(BF16)
+
+
+def attention_forward(where, h1_rel, w_query, keys_values, cosine, sine, seg_query, seg_key):
+    rows, width = h1_rel.shape
+    seq_len = keys_values.shape[0]
+    cols = width // N_SHARD
+    heads = cols // HEAD
+
+    def whole(shape):
+        return pl.BlockSpec(shape, lambda j, w: (0,) * len(shape))
+
+    weight = pl.BlockSpec((cols, cols), lambda j, w: (0, w[0] ^ j))
+    part = pl.BlockSpec((rows, cols), lambda j, w: (0, j))
+    return pl.pallas_call(
+        attention_forward_body,
+        grid_spec=pltpu.PrefetchScalarGridSpec(
+            num_scalar_prefetch=1,
+            grid=(N_SHARD,),
+            in_specs=[
+                whole((rows, width)), weight, weight, weight, weight,
+                pl.BlockSpec((seq_len, HEAD), lambda j, w: (0, (w[0] ^ j) // 2)),
+                pl.BlockSpec((seq_len, HEAD), lambda j, w: (0, KVH + (w[0] ^ j) // 2)),
+                whole((rows, HEAD)), whole((rows, HEAD)), whole((rows, 1)), whole((1, seq_len)),
+            ],
+            out_specs=[part, pl.BlockSpec((heads, rows, seq_len), lambda j, w: (j, 0, 0)), part],
+            scratch_shapes=[pltpu.VMEM((rows, seq_len), F32)],
+        ),
+        out_shape=[
+            jax.ShapeDtypeStruct((rows, width), BF16),
+            jax.ShapeDtypeStruct((HQ, rows, seq_len), BF16),
+            jax.ShapeDtypeStruct((rows, width), BF16),
+        ],
+        compiler_params=pltpu.CompilerParams(vmem_limit_bytes=40 * MEBIBYTE),
+        cost_estimate=pl.CostEstimate(flops=5 * 10**9, bytes_accessed=2 * 10**7, transcendentals=3 * 10**6),
+        name="attention_forward",
+    )(where, h1_rel, *w_query, keys_values, keys_values, cosine, sine, seg_query, seg_key)
+
+
+def attention_backward_body(
+    where_ref, branch_ref, out0, out1, out2, out3, attended_ref, query_ref, prob_ref, key_ref, value_ref,
+    w0, w1, w2, w3, cos_ref, sin_ref,
+    dq_out, dk_out, dv_out, dh_out, dh_acc, dk_acc, dv_acc, da_ref, stack_ref,
+):
+    step = pl.program_id(0)
+    depth = w0.shape[0]
+    rows = branch_ref.shape[0]
+
+    for j, weight in enumerate((out0, out1, out2, out3)):
+
+        @pl.when(step == j)
+        def _(weight=weight):
+            da_ref[...] = dot_nt(branch_ref[...], weight[...]).astype(BF16)
+
+    @pl.when(step % 2 == 0)
+    def _():
+        dk_acc[...] = jnp.zeros_like(dk_acc)
+        dv_acc[...] = jnp.zeros_like(dv_acc)
+
+    @pl.when(step == 0)
+    def _():
+        dh_acc[...] = jnp.zeros_like(dh_acc)
+
+    d_pre = []
+    for h in range(depth // HEAD):
+        cols = slice(h * HEAD, (h + 1) * HEAD)
+        d_att = da_ref[:, cols]
+        probs = prob_ref[h]
+        delta = jnp.sum(d_att.astype(F32) * attended_ref[:, cols].astype(F32), -1, keepdims=True)
+        d_probs = dot_nt(d_att, value_ref[...])
+        d_scores = (probs.astype(F32) * ((d_probs - delta) * HEAD ** (-0.5))).astype(BF16)
+        stack_ref[h * rows : (h + 1) * rows, :] = d_scores
+        d_query = dot_nn(d_scores, key_ref[...])
+        d_pre.append(turn(d_query, cos_ref[...], -sin_ref[...]).astype(BF16))
+        dk_acc[...] += dot_tn(query_ref[:, cols], d_scores)
+        dv_acc[...] += dot_tn(d_att, probs)
+    d_pre = jnp.concatenate(d_pre, 1)
+    dq_out[...] = d_pre
+    for j, weight in enumerate((w0, w1, w2, w3)):
+        dh_acc[:, j * depth : (j + 1) * depth] += dot_nt(d_pre, weight[...])
+
+    @pl.when(step % 2 == 1)
+    def _():
+        dk_out[...] = dk_acc[...].T.astype(BF16)
+        dv_out[...] = dv_acc[...].T.astype(BF16)
+
+    @pl.when(step == N_SHARD - 1)
+    def _():
+        dh_out[...] = dh_acc[...]
+
+
+def attention_backward(where, branch, w_out, attended, queries, probs, keys_values, w_query, cosine, sine):
+    rows, width = branch.shape
+    seq_len = keys_values.shape[0]
+    cols = width // N_SHARD
+    heads = cols // HEAD
+
+    def whole(shape):
+        return pl.BlockSpec(shape, lambda j, w: (0,) * len(shape))
+
+    weight = pl.BlockSpec((cols, cols), lambda j, w: (0, w[0] ^ j))
+    part = pl.BlockSpec((rows, cols), lambda j, w: (0, j))
+    head_part = pl.BlockSpec((seq_len, HEAD), lambda j, w: (0, (w[0] ^ j) // 2))
+    return pl.pallas_call(
+        attention_backward_body,
+        grid_spec=pltpu.PrefetchScalarGridSpec(
+            num_scalar_prefetch=1,
+            grid=(N_SHARD,),
+            in_specs=[whole((rows, width))] + [whole((cols, width))] * 4 + [
+                part, part, pl.BlockSpec((heads, rows, seq_len), lambda j, w: (j, 0, 0)),
+                head_part,
+                pl.BlockSpec((seq_len, HEAD), lambda j, w: (0, KVH + (w[0] ^ j) // 2)),
+                weight, weight, weight, weight, whole((rows, HEAD)), whole((rows, HEAD)),
+            ],
+            out_specs=[
+                pl.BlockSpec((rows, cols), lambda j, w: (0, w[0] ^ j)),
+                head_part, head_part, whole((rows, width)),
+            ],
+            scratch_shapes=[
+                pltpu.VMEM((rows, width), F32),
+                pltpu.VMEM((HEAD, seq_len), F32),
+                pltpu.VMEM((HEAD, seq_len), F32),
+                pltpu.VMEM((rows, cols), BF16),
+                pltpu.VMEM((heads * rows, seq_len), BF16),
+            ],
+        ),
+        out_shape=[
+            jax.ShapeDtypeStruct((rows, width), BF16),
+            jax.ShapeDtypeStruct((seq_len, KVH * HEAD), BF16),
+            jax.ShapeDtypeStruct((seq_len, KVH * HEAD), BF16),
+            jax.ShapeDtypeStruct((rows, width), F32),
+        ],
+        compiler_params=pltpu.CompilerParams(vmem_limit_bytes=48 * MEBIBYTE),
+        cost_estimate=pl.CostEstimate(flops=8 * 10**9, bytes_accessed=3 * 10**7, transcendentals=0),
+        name="attention_backward",
+    )(where, branch, *w_out, attended, queries, probs, keys_values, keys_values, *w_query, cosine, sine)
+
+
+def expert_body(
+    where_ref, h2_ref, dy_ref, router_ref, gate_own, up_own, down_own, gate_far, up_far, down_far,
+    message_out, mixed_out, da_out, db_out, act_out, gates_ref, dh_acc, y_acc, gg_acc,
+):
+    e = pl.program_id(0)
+    f = pl.program_id(1)
+    rows, width = h2_ref.shape
+    lane = lax.broadcasted_iota(jnp.int32, (rows, LANES), 1)
+
+    @pl.when((e == 0) & (f == 0))
+    def _():
+        named = dy_ref[:, width:].astype(F32) > 0.5
+        logits = jnp.where(named, dot_nn(h2_ref[...], router_ref[...]), MASKED_SCORE)
+        top = jnp.max(logits, -1, keepdims=True)
+        weights = jnp.where(named, jnp.exp(logits - top), 0.0)
+        gates_ref[...] = weights / jnp.sum(weights, -1, keepdims=True)
+        dh_acc[...] = jnp.zeros_like(dh_acc)
+        y_acc[...] = jnp.zeros_like(y_acc)
+        gg_acc[...] = jnp.zeros_like(gg_acc)
+
+    here = lane == (where_ref[0] ^ e)
+
+    def work(gate_ref, up_ref, down_ref):
+        gate = jnp.sum(jnp.where(here, gates_ref[...], 0.0), -1, keepdims=True)
+        h2 = h2_ref[...]
+        a = dot_nn(h2, gate_ref[...])
+        b = dot_nn(h2, up_ref[...])
+        d_plain = dot_nt(dy_ref[:, :width], down_ref[...])
+        sigmoid = 1.0 / (1.0 + jnp.exp(-a))
+        silu = a * sigmoid
+        act = silu * b
+        gate_grad = jnp.sum(act * d_plain, -1, keepdims=True)
+        gg_acc[...] += jnp.where(here, gate_grad, 0.0)
+        d_act = d_plain * gate
+        d_a = (d_act * b * (sigmoid + silu * (1.0 - sigmoid))).astype(BF16)
+        d_b = (d_act * silu).astype(BF16)
+        scaled = (act * gate).astype(BF16)
+        da_out[...] = d_a
+        db_out[...] = d_b
+        act_out[...] = scaled
+        dh_acc[...] += dot_nt(d_a, gate_ref[...]) + dot_nt(d_b, up_ref[...])
+        y_acc[...] += dot_nn(scaled, down_ref[...])
+
+    @pl.when(e == 0)
+    def _():
+        work(gate_own, up_own, down_own)
+
+    @pl.when(e == 1)
+    def _():
+        work(gate_far, up_far, down_far)
+
+    @pl.when((e == pl.num_programs(0) - 1) & (f == pl.num_programs(1) - 1))
+    def _():
+        message_out[:, :width] = dh_acc[...].astype(BF16)
+        high = gg_acc[...].astype(BF16).astype(F32)
+        low = pltpu.roll(gg_acc[...] - high, N_EXPERT, 1)
+        message_out[:, width:] = (high + low).astype(BF16)
+        mixed_out[...] = y_acc[...].astype(BF16)
+
+
+def expert_block(where, h2, dy_routes, router, own, far):
+    rows, width = h2.shape
+    hidden = own[0].shape[1]
+    chunk = 256
+    chunks = hidden // chunk
+
+    def whole(shape):
+        return pl.BlockSpec(shape, lambda e, f, w: (0,) * len(shape))
+
+    own_step = lambda e, f: jnp.where(e == 0, f, chunks - 1)
+    far_step = lambda e, f: jnp.where(e == 0, 0, f)
+    own_in = pl.BlockSpec((width, chunk), lambda e, f, w: (0, own_step(e, f)))
+    own_down = pl.BlockSpec((chunk, width), lambda e, f, w: (own_step(e, f), 0))
+    far_in = pl.BlockSpec((width, chunk), lambda e, f, w: (0, far_step(e, f)))
+    far_down = pl.BlockSpec((chunk, width), lambda e, f, w: (far_step(e, f), 0))
+    part = pl.BlockSpec((rows, chunk), lambda e, f, w: (0, e * chunks + f))
+    return pl.pallas_call(
+        expert_body,
+        grid_spec=pltpu.PrefetchScalarGridSpec(
+            num_scalar_prefetch=1,
+            grid=(2, chunks),
+            in_specs=[
+                whole((rows, width)), whole(dy_routes.shape), whole(router.shape),
+                own_in, own_in, own_down, far_in, far_in, far_down,
+            ],
+            out_specs=[whole((rows, width + LANES)), whole((rows, width)), part, part, part],
+            scratch_shapes=[
+                pltpu.VMEM((rows, LANES), F32),
+                pltpu.VMEM((rows, width), F32),
+                pltpu.VMEM((rows, width), F32),
+                pltpu.VMEM((rows, LANES), F32),
+            ],
+        ),
+        out_shape=[
+            jax.ShapeDtypeStruct((rows, width + LANES), BF16),
+            jax.ShapeDtypeStruct((rows, width), BF16),
+            jax.ShapeDtypeStruct((rows, 2 * hidden), BF16),
+            jax.ShapeDtypeStruct((rows, 2 * hidden), BF16),
+            jax.ShapeDtypeStruct((rows, 2 * hidden), BF16),
+        ],
+        compiler_params=pltpu.CompilerParams(vmem_limit_bytes=40 * MEBIBYTE),
+        cost_estimate=pl.CostEstimate(flops=8 * 10**9, bytes_accessed=2 * 10**7, transcendentals=4 * 10**5),
+        name="expert_block",
+    )(where, h2, dy_routes, router, *own, *far)
+
+
+def summed_products_body(where_ref, *refs, parts, sets):
+    lefts = refs[:parts]
+    rights = refs[parts : parts * (1 + sets)]
+    outs = refs[parts * (1 + sets) :]
+    for k in range(sets):
+        total = dot_tn(lefts[0][...], rights[k * parts][...])
+        for j in range(1, parts):
+            total = total + dot_tn(lefts[j][...], rights[k * parts + j][...])
+        out = outs[k]
+        if len(out.shape) == 3:
+            pieces = out.shape[0]
+            deep = out.shape[1]
+            for piece in range(pieces):
+                out[where_ref[0] ^ piece] = total[piece * deep : (piece + 1) * deep].astype(out.dtype)
+        else:
+            out[...] = total.astype(out.dtype)
+
+
+def summed_products(where, lefts, right_sets, grid, left_spec, right_spec, out_spec, out_shape, name):
+    parts = len(lefts)
+    sets = len(right_sets)
+    return pl.pallas_call(
+        functools.partial(summed_products_body, parts=parts, sets=sets),
+        grid_spec=pltpu.PrefetchScalarGridSpec(
+            num_scalar_prefetch=1,
+            grid=grid,
+            in_specs=[left_spec] * parts + [right_spec] * (parts * sets),
+            out_specs=[out_spec] * sets,
+        ),
+        out_shape=[jax.ShapeDtypeStruct(out_shape, BF16)] * sets,
+        compiler_params=pltpu.CompilerParams(vmem_limit_bytes=48 * MEBIBYTE),
+        cost_estimate=pl.CostEstimate(flops=3 * 10**9, bytes_accessed=10**7, transcendentals=0),
+        name=name,
+    )(where, *lefts, *[member for members in right_sets for member in members])
+
+
+def sum_over_planes(pieces):
+    shape = pieces.shape[1:]
+    low = pieces.reshape((4, 2) + shape)
+    kept = low[:, 0].astype(F32) + swap(low[:, 1], 1, 0).astype(F32)
+    kept = kept.astype(BF16).reshape((2, 2) + shape)
+    kept = kept[:, 0].astype(F32) + swap(kept[:, 1], 2, 0).astype(F32)
+    kept = kept.astype(BF16)
+    own = (kept[0].astype(F32) + swap(kept[1], 4, 0).astype(F32)).astype(BF16)
+    two = jnp.stack([own, swap(own, 4, 0)])
+    four = jnp.stack([two, swap(two, 2, 0)], 1).reshape((4,) + shape)
+    return four, swap(four, 1, 0)
+
+
+def reorder_body(where_ref, even_ref, odd_ref, out_ref):
+    place = where_ref[0] ^ pl.program_id(0)
+
+    @pl.when(place % 2 == 0)
+    def _():
+        out_ref[...] = even_ref[...].astype(F32)
+
+    @pl.when(place % 2 == 1)
+    def _():
+        out_ref[...] = odd_ref[...].astype(F32)
+
+
+def reorder(where, even, odd):
+    shape = even.shape[1:]
+    spec = pl.BlockSpec((1,) + shape, lambda b, w: ((w[0] ^ b) // 2, 0, 0))
+    return pl.pallas_call(
+        reorder_body,
+        grid_spec=pltpu.PrefetchScalarGridSpec(
+            num_scalar_prefetch=1,
+            grid=(N_EXPERT,),
+            in_specs=[spec, spec],
+            out_specs=pl.BlockSpec((1,) + shape, lambda b, w: (b, 0, 0)),
+        ),
+        out_shape=jax.ShapeDtypeStruct((N_EXPERT,) + shape, F32),
+        name="reorder",
+    )(where, even, odd).reshape(N_EXPERT * shape[0], shape[1])
+
+
+def fetch_far(mine, core):
+    half = mine.shape[0] // 2
+    part = swap(lax.dynamic_slice_in_dim(mine, core * half, half, 0), 1, 0)
+    return rejoin(part, swap(part, 0, 1), core == 0)
+
+
+def expert_weight_sums(send, keep, axis, core):
+    received = swap(send, 0, 1)
+    half = send.shape[axis] // 2
+    cut = lambda a, i: lax.slice_in_dim(a, i * half, (i + 1) * half, axis=axis).astype(F32)
+    for_far = (cut(keep, 1) + cut(received, 1)).astype(BF16)
+    total = cut(keep, 0) + cut(received, 0) + swap(for_far, 1, 0).astype(F32)
+    total = total.astype(BF16)
+    total = (total.astype(F32) + swap(total, 0, 2).astype(F32)).astype(BF16)
+    return rejoin(total, swap(total, 0, 1), core == 0).astype(F32)[None]
+
+
+def on_device_rings(
+    hidden_in, segment_ids, routes, attn_gain, moe_gain, w_query, w_key, w_value, w_out, w_router,
+    expert_gate, expert_up, expert_down, out_grad,
+):
+    rows, width = hidden_in.shape
+    experts = w_router.shape[1]
+    shard = lax.axis_index("shard")
+    expert = lax.axis_index("expert")
+    core = shard % 2
+    where_shard = shard.astype(jnp.int32)[None]
+    where_expert = expert.astype(jnp.int32)[None]
+    where_core = core.astype(jnp.int32)[None]
+    where_far_core = 1 - where_core
+    block = width // N_SHARD
+    low = KVH * HEAD
+
+    small = jnp.concatenate(
+        [w_router, attn_gain[:, None], moe_gain[:, None], jnp.zeros((block, LANES - experts - 2), BF16)], 1
+    )
+    packed = gather_shards(jnp.concatenate([w_key, w_value, small], 1))
+    query_w = gather_shards(w_query)
+    out_w = gather_shards(w_out)
+    mask = (routes[:, :, None] == jnp.arange(LANES, dtype=jnp.int32)[None, None, :]).any(1)
+    dy_routes = [jnp.concatenate([out_grad, mask.astype(BF16)], 1)]
+    for _ in range(3):
+        dy_routes.append(next_plane(dy_routes[-1]))
+    own = (expert_gate[0], expert_up[0], expert_down[0])
+    far = tuple(fetch_far(member, core) for member in own)
+
+    inputs = hidden_in.astype(F32)
+    factor_attn = lax.rsqrt(jnp.mean(inputs * inputs, -1, keepdims=True) + EPSILON)
+    unit_rel = jnp.concatenate(
+        xor_blocks([inputs[:, j * block : (j + 1) * block] for j in range(4)], shard), 1
+    ) * factor_attn
+    gain_rel = jnp.concatenate([member[:, 2 * low + experts] for member in packed]).astype(F32)
+    h1_rel = (unit_rel * gain_rel).astype(BF16)
+    key_value_w = [member[:, : 2 * low] for member in packed]
+    pre = sum(dot_nn(h1_rel[:, j * block : (j + 1) * block], key_value_w[j]) for j in range(4))
+    positions = shard * rows + jnp.arange(rows, dtype=jnp.int32)
+    cosine, sine = rope_tables(positions, HEAD)
+    key_local = rotate(pre[:, :low], cosine, sine, HEAD)
+    key_value = jnp.concatenate([key_local, pre[:, low:]], 1).astype(BF16)
+    keys_values = jnp.concatenate(xor_blocks(gather_shards(key_value), shard), 0)
+    cosine_row = jnp.concatenate([cosine, cosine], 1)
+    sine_row = jnp.concatenate([-sine, sine], 1)
+    seg_query = lax.dynamic_slice_in_dim(segment_ids, shard * rows, rows)[:, None]
+    queries, probs, attended = attention_forward(
+        where_shard, h1_rel, query_w, keys_values, cosine_row, sine_row, seg_query, segment_ids[None, :]
+    )
+    mid_state = inputs + sum(
+        dot_nn(attended[:, j * block : (j + 1) * block], out_w[j]) for j in range(4)
+    )
+    factor_moe = lax.rsqrt(jnp.mean(mid_state * mid_state, -1, keepdims=True) + EPSILON)
+    unit_moe = mid_state * factor_moe
+    small_true = jnp.concatenate(xor_blocks([member[:, 2 * low :] for member in packed], shard), 0)
+    gain_moe = small_true[:, experts + 1].astype(F32)
+    router_pad = jnp.where(jnp.arange(LANES)[None, :] < experts, small_true, 0)
+    router = small_true[:, :experts].astype(F32)
+    h2 = [(unit_moe * gain_moe).astype(BF16)]
+
+    h1_rows = [h1_rel[:, :block]] + [swap(h1_rel[:, j * block : (j + 1) * block], 0, j) for j in (1, 2, 3)]
+    att_rows = [attended[:, :block]] + [
+        swap(attended[:, j * block : (j + 1) * block], 0, j) for j in (1, 2, 3)
+    ]
+
+    for _ in range(3):
+        h2.append(next_plane(h2[-1]))
+    done = [None] * 4
+    add = lambda a, b: (a.astype(F32) + b.astype(F32)).astype(BF16)
+    done[0] = expert_block(where_expert, h2[0], dy_routes[0], router_pad, own, far)
+    message = None
+    mixed = None
+    for j in (1, 2, 3):
+        done[j] = expert_block(where_expert, h2[j], dy_routes[j], router_pad, own, far)
+        message = next_plane(done[j][0] if j == 1 else add(done[j][0], message))
+        mixed = next_plane(done[j][1] if j == 1 else add(done[j][1], mixed))
+    total = done[0][0].astype(F32) + message.astype(F32)
+    layer_out = (mid_state + done[0][1].astype(F32) + mixed.astype(F32)).astype(BF16)
+
+    hidden = own[0].shape[1]
+    deep = width // 2
+
+    def in_grads(where):
+        return summed_products(
+            where, h2, [[done[j][2] for j in range(4)], [done[j][3] for j in range(4)]], (2,),
+            pl.BlockSpec((rows, deep), lambda i, w: (0, w[0])),
+            pl.BlockSpec((rows, hidden), lambda i, w: (0, i)),
+            pl.BlockSpec((deep, hidden), lambda i, w: (0, i)),
+            (deep, 2 * hidden), "expert_in_grads",
+        )
+
+    def down_grads(where):
+        return summed_products(
+            where, [done[j][4] for j in range(4)], [dy_routes], (2,),
+            pl.BlockSpec((rows, hidden // 2), lambda i, w: (0, 2 * i + w[0])),
+            pl.BlockSpec((rows, width), lambda i, w: (0, 0)),
+            pl.BlockSpec((hidden // 2, width), lambda i, w: (i, 0)),
+            (hidden, width), "expert_down_grads",
+        )
+
+    (down_send,) = down_grads(where_far_core)
+    gate_send, up_send = in_grads(where_far_core)
+    (down_keep,) = down_grads(where_core)
+    gate_keep, up_keep = in_grads(where_core)
+    down_sum = expert_weight_sums(down_send, down_keep, 0, core)
+    gate_sum = expert_weight_sums(gate_send, gate_keep, 1, core)
+    up_sum = expert_weight_sums(up_send, up_keep, 1, core)
+
+    named = mask[:, :experts]
+    logits = jnp.where(named, dot_nn(h2[0], router_pad[:, :experts]), MASKED_SCORE)
+    weights = jnp.where(named, jnp.exp(logits - jnp.max(logits, -1, keepdims=True)), 0.0)
+    gate = weights / jnp.sum(weights, -1, keepdims=True)
+    gate_grad = total[:, width : width + experts] + total[:, width + experts : width + 2 * experts]
+    d_logits = gate * (gate_grad - jnp.sum(gate * gate_grad, -1, keepdims=True))
+    d_h2 = total[:, :width] + jnp.dot(d_logits, router.T, precision=HIGHEST)
+    router_grad = jnp.dot(d_logits.T, h2[0].astype(F32), precision=HIGHEST)
+    d_mid_norm, gain_moe_grad = norm_backward(d_h2, unit_moe, factor_moe, gain_moe)
+    d_mid = out_grad.astype(F32) + d_mid_norm
+    d_branch = d_mid.astype(BF16)
+    branches = gather_shards(d_branch)
+
+    def mixer_grads(lefts, rights, name):
+        n = rights[0].shape[1]
+        (pieces,) = summed_products(
+            where_expert, lefts, [rights], (1,),
+            pl.BlockSpec((rows, block), lambda i, w: (0, 0)),
+            pl.BlockSpec((rows, n), lambda i, w: (0, 0)),
+            pl.BlockSpec((N_EXPERT, block // N_EXPERT, n), lambda i, w: (0, 0, 0)),
+            (N_EXPERT, block // N_EXPERT, n), name,
+        )
+        even, odd = sum_over_planes(pieces)
+        return reorder(where_expert, even, odd)
+
+    out_w_grad = mixer_grads(att_rows, branches, "w_out_grad")
+
+    d_q_pre, d_key_part, d_value_part, d_normed = attention_backward(
+        where_shard, d_branch, out_w, attended, queries, probs, keys_values, query_w, cosine_row, sine_row
+    )
+    d_parts = jnp.concatenate([d_key_part, d_value_part], 1).reshape(N_SHARD, rows, 2 * low)
+    d_rel = xor_blocks([d_parts[j] for j in range(4)], shard)
+    from_core = swap(jnp.stack([d_rel[1], d_rel[3]]), 0, 1)
+    d_far = add(d_rel[2], from_core[1])
+    d_key_value = d_rel[0].astype(F32) + from_core[0].astype(F32) + swap(d_far, 0, 2).astype(F32)
+    d_k_pre = rotate(d_key_value[:, :low], cosine, -sine, HEAD)
+    d_kv_pre = jnp.concatenate([d_k_pre, d_key_value[:, low:]], 1).astype(BF16)
+    d_pre = gather_shards(jnp.concatenate([d_q_pre, d_kv_pre], 1))
+    in_grad = mixer_grads(h1_rows, d_pre, "w_in_grads")
+    d_normed = d_normed + jnp.concatenate([dot_nt(d_kv_pre, member) for member in key_value_w], 1)
+    d_input_norm, gain_attn_grad = norm_backward(d_normed, unit_rel, factor_attn, gain_rel)
+    d_input_norm = jnp.concatenate(
+        xor_blocks([d_input_norm[:, j * block : (j + 1) * block] for j in range(4)], shard), 1
+    )
+    input_grad = d_mid + d_input_norm
+
+    rest = jnp.concatenate([gain_moe_grad[None], router_grad, jnp.zeros((6, width), F32)], 0)
+    rest = xor_blocks([rest[:, j * block : (j + 1) * block] for j in range(4)], shard)
+    pieces = [
+        jnp.concatenate([gain_attn_grad[None, j * block : (j + 1) * block], rest[j]], 0) for j in range(4)
+    ]
+    from_core = swap(jnp.stack([pieces[1], pieces[3]]), 0, 1)
+    sums = pieces[0] + from_core[0] + swap(pieces[2] + from_core[1], 0, 2)
+    for bit in (1, 2, 4):
+        sums = sums + swap(sums, bit, 0)
+    return (
+        layer_out,
+        input_grad,
+        sums[0],
+        sums[1],
+        in_grad[:, :width],
+        in_grad[:, width : width + low],
+        in_grad[:, width + low :],
+        out_w_grad,
+        sums[2 : 2 + experts].T,
+        gate_sum,
+        up_sum,
+        down_sum,
+    )
+
+
+def on_device(hidden_in, segment_ids, routes, *rest):
+    rows = hidden_in.shape[0]
+    experts = rest[6].shape[1]
+    capacity = rows * routes.shape[1] * 2 // experts
+    shape = (lax.axis_size("expert"), lax.axis_size("shard"))
+    if shape == (N_EXPERT, N_SHARD) and experts == N_EXPERT and capacity == rows:
+        return on_device_rings(hidden_in, segment_ids, routes, *rest)
+    return on_device_routed(hidden_in, segment_ids, routes, *rest)
+
+
 def solution(mesh):
     placed = (
         P(("expert", "shard"), None),

time: 1440 us -> 635 us (0.44)
  blocking collectives: 395 us -> 0 us
  waiting for transfers between devices: 645 us -> 314 us
  matrix products: 175 us -> 15.1 us
  Pallas kernels: 0 us -> 136 us
  local copies, waits for them, and re-layouts: 118 us -> 43.9 us
  starting transfers between devices: 10.3 us -> 53.5 us
    psum x2 -> x0, waiting for transfers between devices: 415 us -> none  [the longest x1 302 us: on_device(): lax.psum((partial_sums[0], partial_sums[1], partial_sums[2], partial_sums...]
    ppermute x0 -> x73, waiting for transfers between devices: none -> 314 us  [the longest x61 235 us: swap(): return lax.ppermute(values, AXES, pairs)]
    all_to_all x2 -> x0, blocking collectives: 286 us -> none  [the longest x1 144 us: on_device(): lax.all_to_all(outgoing, 'expert', split_axis=0, concat_axis=0, tiled=True)]
    all_to_all x2 -> x0, waiting for transfers between devices: 229 us -> none  [the longest x1 127 us: on_device(): lax.all_to_all(d_rows, 'expert', split_axis=0, concat_axis=0, tiled=True)]
    dot_general x30 -> x15, matrix products: 175 us -> 15.1 us  [the longest x9 8.66 us: dot_nn(): lax.dot_general(left, right, (((1,), (0,)), ((), ())), preferred_element_...]
    pallas_call x0 -> x14, Pallas kernels: none -> 136 us  [the longest x4 59.5 us: expert_block(): pl.pallas_call(expert_body, grid_spec=pltpu.PrefetchScalarGridSpec(num_sc...]
    all_gather x7 -> x0, blocking collectives: 66.3 us -> none  [the longest x1 13.6 us: on_device(): lax.all_gather(w_value, 'shard', axis=0, tiled=True)]
    gather x5 -> x0, local copies, waits for them, and re-layouts: 56.2 us -> none  [the longest x1 15.8 us: on_device(): jnp.take(grad_out, source // top_count, axis=0) * gate_slots[:, None]]
  transfers between devices with their start and end apart: 8 -> 73, of which waited for: 4 -> 33; matrix products, arithmetic and copies ran while one was open for 12% -> 15% of each run, Pallas kernels for 0% -> 21%
where the time goes in v1:
time: 635 us; the launch traced here: 626 us
  waiting for transfers between devices  314 us (49%)
  Pallas kernels  136 us (21%)
  other arithmetic  59.9 us (9%)
  starting transfers between devices  53.5 us (8%)
  local copies, waits for them, and re-layouts  43.9 us (7%)
  matrix products  15.1 us (2%)
    ppermute x61, waiting for transfers between devices, swap(): return lax.ppermute(values, AXES, pairs)  235 us
    ppermute x12, waiting for transfers between devices, next_plane(): return lax.ppermute(values, AXES, pairs)  78.3 us
    pallas_call x4, Pallas kernels, expert_block(): pl.pallas_call(expert_body, grid_spec=pltpu.PrefetchScalarGridSpec(num_sc...  59.5 us
    ppermute x61, starting transfers between devices, swap(): return lax.ppermute(values, AXES, pairs)  42.6 us
    pallas_call x6, Pallas kernels, summed_products(): pl.pallas_call(functools.partial(summed_products_body, parts=parts, sets=...  33.7 us
    unnamed x289, local copies, waits for them, and re-layouts  17.5 us
    pallas_call x1, Pallas kernels, attention_backward(): pl.pallas_call(attention_backward_body, grid_spec=pltpu.PrefetchScalarGri...  16.6 us
    pallas_call x1, Pallas kernels, attention_forward(): pl.pallas_call(attention_forward_body, grid_spec=pltpu.PrefetchScalarGrid...  14.7 us
  transfers between devices with their start and end apart: 73, of which 33 were waited for; matrix products, arithmetic and copies ran while one was open for 15% of the time, Pallas kernels for 21%

profile of v1, /device:TPU:0, one launch (start us, length us, event | category | flops | bytes accessed | tf_op | source)
XLA Modules:
  0.0 625.5 jit_solution(5445213421959268521)
XLA Ops:
  38.0 8.5 %collective-permute-done.21.dy_ref.refs_5_ = bf16[256,1664]{1,0:T(8,128)(2,1)S(1)} collective-permute-done((bf16[256,1664]{1,0:T(8,128)(2,1)S(1)}, bf16[256,1664]{1,0:T(8,128)(2,1)S(1)}, u32[]{:S(2)}, u32[]{:S(2)}) %collective-permute-start.21) | collective-permute-done | bytes 852000 | tf_op jit(solution)/shard_map/ppermute | solution.py:352
  47.9 23.2 %collective-permute-done.10.out2 = bf16[384,1536]{1,0:T(8,128)(2,1)} collective-permute-done((bf16[384,1536]{1,0:T(8,128)(2,1)}, bf16[384,1536]{1,0:T(8,128)(2,1)}, u32[]{:S(2)}, u32[]{:S(2)}) %collective-permute-start.10) | collective-permute-done | bytes 1179680 | tf_op jit(solution)/shard_map/ppermute | solution.py:343
  83.1 14.7 %attention_forward.1 = (bf16[256,1536]{1,0:T(8,128)(2,1)S(1)}, bf16[12,256,1024]{2,1,0:T(8,128)(2,1)}, bf16[256,1536]{1,0:T(8,128)(2,1)S(1)}) custom-call(s32[1]{0:T(128)} %bitcast.where_ref, bf16[256,1536]{1,0:T(8,128)(2,1)S(1)} %multiply_convert_fusion.1.h1_ref, bf16[384,1536]{1,0:T(8,128)(2,1)} %w0.3, bf16[384,1536]{1,0:T(8,128)(2,1)} %collective-permute-done.3.w1, ...), custom_call_target="tpu_custom_call" | custom-call | flops 5000000000 | bytes 20000000 | tf_op jit(solution)/shard_map/attention_forward/pallas_call | solution.py:433
  99.9 5.8 collective-permute-done.12
  105.7 25.3 %collective-permute-done.14 = bf16[768,768]{1,0:T(8,128)(2,1)S(1)} collective-permute-done((bf16[768,768]{1,0:T(8,128)(2,1)S(1)}, bf16[768,768]{1,0:T(8,128)(2,1)S(1)}, u32[]{:S(2)}, u32[]{:S(2)}) %collective-permute-start.14) | collective-permute-done | bytes 1179680 | tf_op jit(solution)/shard_map/ppermute | solution.py:343
  131.0 24.9 %collective-permute-done.16 = bf16[384,1536]{1,0:T(8,128)(2,1)S(1)} collective-permute-done((bf16[384,1536]{1,0:T(8,128)(2,1)S(1)}, bf16[384,1536]{1,0:T(8,128)(2,1)S(1)}, u32[]{:S(2)}, u32[]{:S(2)}) %collective-permute-start.16) | collective-permute-done | bytes 1179680 | tf_op jit(solution)/shard_map/ppermute | solution.py:343
  170.6 14.7 %expert_block.4 = (bf16[256,1664]{1,0:T(8,128)(2,1)S(1)}, bf16[256,1536]{1,0:T(8,128)(2,1)S(1)}, bf16[256,1536]{1,0:T(8,128)(2,1)S(1)}, bf16[256,1536]{1,0:T(8,128)(2,1)S(1)}, bf16[256,1536]{1,0:T(8,128)(2,1)S(1)}) custom-call(s32[1]{0:T(128)} %bitcast.3.where_ref, bf16[256,1536]{1,0:T(8,128)(2,1)S(1)} %multiply_convert_fusion.h2_ref.refs_0_, ...), custom_call_target="tpu_custom_call" | custom-call | flops 8000000000 | bytes 20000000 | tf_op jit(solution)/shard_map/expert_block/pallas_call | solution.py:633
  188.1 8.3 %collective-permute-done.18.h2_ref.refs_1_ = bf16[256,1536]{1,0:T(8,128)(2,1)S(1)} collective-permute-done((bf16[256,1536]{1,0:T(8,128)(2,1)S(1)}, bf16[256,1536]{1,0:T(8,128)(2,1)S(1)}, u32[]{:S(2)}, u32[]{:S(2)}) %collective-permute-start.18) | collective-permute-done | bytes 786464 | tf_op jit(solution)/shard_map/ppermute | solution.py:352
  196.4 14.9 %expert_block.7 = (bf16[256,1664]{1,0:T(8,128)(2,1)S(1)}, bf16[256,1536]{1,0:T(8,128)(2,1)S(1)}, bf16[256,1536]{1,0:T(8,128)(2,1)S(1)}, bf16[256,1536]{1,0:T(8,128)(2,1)S(1)}, bf16[256,1536]{1,0:T(8,128)(2,1)S(1)}) custom-call(s32[1]{0:T(128)} %bitcast.3.where_ref, bf16[256,1536]{1,0:T(8,128)(2,1)S(1)} %collective-permute-done.18.h2_ref.refs_1_, ...), custom_call_target="tpu_custom_call" | custom-call | flops 8000000000 | bytes 20000000 | tf_op jit(solution)/shard_map/expert_block/pallas_call | solution.py:633
  218.4 15.0 %expert_block.6 = (bf16[256,1664]{1,0:T(8,128)(2,1)S(1)}, bf16[256,1536]{1,0:T(8,128)(2,1)S(1)}, bf16[256,1536]{1,0:T(8,128)(2,1)S(1)}, bf16[256,1536]{1,0:T(8,128)(2,1)S(1)}, bf16[256,1536]{1,0:T(8,128)(2,1)S(1)}) custom-call(s32[1]{0:T(128)} %bitcast.3.where_ref, bf16[256,1536]{1,0:T(8,128)(2,1)S(1)} %collective-permute-done.19.h2_ref.refs_2_, ...), custom_call_target="tpu_custom_call" | custom-call | flops 8000000000 | bytes 20000000 | tf_op jit(solution)/shard_map/expert_block/pallas_call | solution.py:633
  238.2 15.4 %collective-permute-done.24 = bf16[256,1536]{1,0:T(8,128)(2,1)} collective-permute-done((bf16[256,1536]{1,0:T(8,128)(2,1)S(1)}, bf16[256,1536]{1,0:T(8,128)(2,1)}, u32[]{:S(2)}, u32[]{:S(2)}) %collective-permute-start.24) | collective-permute-done | bytes 786464 | tf_op jit(solution)/shard_map/ppermute | solution.py:352
  255.1 15.3 %collective-permute-done.20.h2_ref.refs_3_ = bf16[256,1536]{1,0:T(8,128)(2,1)S(1)} collective-permute-done((bf16[256,1536]{1,0:T(8,128)(2,1)S(1)}, bf16[256,1536]{1,0:T(8,128)(2,1)S(1)}, u32[]{:S(2)}, u32[]{:S(2)}) %collective-permute-start.20) | collective-permute-done | bytes 786464 | tf_op jit(solution)/shard_map/ppermute | solution.py:352
  270.4 14.9 %expert_block.5 = (bf16[256,1664]{1,0:T(8,128)(2,1)S(1)}, bf16[256,1536]{1,0:T(8,128)(2,1)S(1)}, bf16[256,1536]{1,0:T(8,128)(2,1)S(1)}, bf16[256,1536]{1,0:T(8,128)(2,1)S(1)}, bf16[256,1536]{1,0:T(8,128)(2,1)S(1)}) custom-call(s32[1]{0:T(128)} %bitcast.3.where_ref, bf16[256,1536]{1,0:T(8,128)(2,1)S(1)} %collective-permute-done.20.h2_ref.refs_3_, ...), custom_call_target="tpu_custom_call" | custom-call | flops 8000000000 | bytes 20000000 | tf_op jit(solution)/shard_map/expert_block/pallas_call | solution.py:633
  289.1 16.5 %collective-permute-done.25 = bf16[256,1536]{1,0:T(8,128)(2,1)} collective-permute-done((bf16[256,1536]{1,0:T(8,128)(2,1)S(1)}, bf16[256,1536]{1,0:T(8,128)(2,1)}, u32[]{:S(2)}, u32[]{:S(2)}) %collective-permute-start.25) | collective-permute-done | bytes 786464 | tf_op jit(solution)/shard_map/ppermute | solution.py:352
  308.0 8.4 %expert_in_grads.3 = (bf16[768,1536]{1,0:T(8,128)(2,1)}, bf16[768,1536]{1,0:T(8,128)(2,1)}) custom-call(s32[1]{0:T(128)S(6)} %sub.39.where_ref, bf16[256,1536]{1,0:T(8,128)(2,1)S(1)} %multiply_convert_fusion.h2_ref.refs_0_, bf16[256,1536]{1,0:T(8,128)(2,1)S(1)} %collective-permute-done.18.h2_ref.refs_1_, bf16[256,1536]{1,0:T(8,128)(2,1)S(1)} %copy-done.24, ...), custom_call_target="tpu_custom_call" | custom-call | flops 3000000000 | bytes 10000000 | tf_op jit(solution)/shard_map/expert_in_grads/pallas_call | solution.py:684
  316.4 7.3 %collective-permute-done.29 = bf16[256,1664]{1,0:T(8,128)(2,1)S(1)} collective-permute-done((bf16[256,1664]{1,0:T(8,128)(2,1)S(1)}, bf16[256,1664]{1,0:T(8,128)(2,1)S(1)}, u32[]{:S(2)}, u32[]{:S(2)}) %collective-permute-start.29) | collective-permute-done | bytes 852000 | tf_op jit(solution)/shard_map/ppermute | solution.py:352
  328.3 16.6 %attention_backward.1 = (bf16[256,1536]{1,0:T(8,128)(2,1)S(1)}, bf16[1024,256]{1,0:T(8,128)(2,1)S(1)}, bf16[1024,256]{1,0:T(8,128)(2,1)S(1)}, f32[256,1536]{1,0:T(8,128)}) custom-call(s32[1]{0:T(128)} %bitcast.where_ref, bf16[256,1536]{1,0:T(8,128)(2,1)S(1)} %fusion.48.branch_ref.refs_4_, bf16[384,1536]{1,0:T(8,128)(2,1)} %out0.1, ...), custom_call_target="tpu_custom_call" | custom-call | flops 8000000000 | bytes 30000000 | tf_op jit(solution)/shard_map/attention_backward/pallas_call | solution.py:522
  355.5 6.6 %collective-permute-done.31 = bf16[256,512]{1,0:T(8,128)(2,1)S(1)} collective-permute-done((bf16[256,512]{1,0:T(8,128)(2,1)S(1)}, bf16[256,512]{1,0:T(8,128)(2,1)S(1)}, u32[]{:S(2)}, u32[]{:S(2)}) %collective-permute-start.31) | collective-permute-done | bytes 262176 | tf_op jit(solution)/shard_map/ppermute | solution.py:343
  374.8 8.8 %expert_in_grads.2 = (bf16[768,1536]{1,0:T(8,128)(2,1)}, bf16[768,1536]{1,0:T(8,128)(2,1)}) custom-call(s32[1]{0:T(128)} %bitcast.47.where_ref, bf16[256,1536]{1,0:T(8,128)(2,1)S(1)} %multiply_convert_fusion.h2_ref.refs_0_, bf16[256,1536]{1,0:T(8,128)(2,1)S(1)} %copy-done.22, bf16[256,1536]{1,0:T(8,128)(2,1)S(1)} %copy-done.25, ...), custom_call_target="tpu_custom_call" | custom-call | flops 3000000000 | bytes 10000000 | tf_op jit(solution)/shard_map/expert_in_grads/pallas_call | solution.py:684
  385.2 5.6 expert_down_grads.2
  400.9 15.8 %collective-permute-done.50.refs_2_ = bf16[256,384]{1,0:T(8,128)(2,1)S(1)} collective-permute-done((bf16[256,384]{1,0:T(8,128)(2,1)S(1)}, bf16[256,384]{1,0:T(8,128)(2,1)S(1)}, u32[]{:S(2)}, u32[]{:S(2)}) %collective-permute-start.50) | collective-permute-done | bytes 196640 | tf_op jit(solution)/shard_map/ppermute | solution.py:343
  422.6 5.8 collective-permute-done.51.refs_3_
  438.2 9.9 %collective-permute-done.55 = bf16[4,48,1536]{2,1,0:T(8,128)(2,1)S(1)} collective-permute-done((bf16[4,48,1536]{2,1,0:T(8,128)(2,1)S(1)}, bf16[4,48,1536]{2,1,0:T(8,128)(2,1)S(1)}, u32[]{:S(2)}, u32[]{:S(2)}) %collective-permute-start.55) | collective-permute-done | bytes 589856 | tf_op jit(solution)/shard_map/ppermute | solution.py:343
  453.1 7.8 %collective-permute-done.41.refs_6_ = bf16[256,2048]{1,0:T(8,128)(2,1)S(1)} collective-permute-done((bf16[256,2048]{1,0:T(8,128)(2,1)S(1)}, bf16[256,2048]{1,0:T(8,128)(2,1)S(1)}, u32[]{:S(2)}, u32[]{:S(2)}) %collective-permute-start.41) | collective-permute-done | bytes 1048608 | tf_op jit(solution)/shard_map/ppermute | solution.py:343
  461.5 13.9 %collective-permute-done.62 = bf16[768,768]{1,0:T(8,128)(2,1)S(1)} collective-permute-done((bf16[768,768]{1,0:T(8,128)(2,1)S(1)}, bf16[768,768]{1,0:T(8,128)(2,1)S(1)}, u32[]{:S(2)}, u32[]{:S(2)}) %collective-permute-start.62) | collective-permute-done | bytes 1179680 | tf_op jit(solution)/shard_map/ppermute | solution.py:343
  492.0 14.4 %collective-permute-done.66 = bf16[768,768]{1,0:T(8,128)(2,1)} collective-permute-done((bf16[768,768]{1,0:T(8,128)(2,1)}, bf16[768,768]{1,0:T(8,128)(2,1)}, u32[]{:S(2)}, u32[]{:S(2)}) %collective-permute-start.66) | collective-permute-done | bytes 1179680 | tf_op jit(solution)/shard_map/ppermute | solution.py:343
  510.7 37.6 %collective-permute-done.43 = bf16[4,48,2048]{2,1,0:T(8,128)(2,1)S(1)} collective-permute-done((bf16[4,48,2048]{2,1,0:T(8,128)(2,1)S(1)}, bf16[4,48,2048]{2,1,0:T(8,128)(2,1)S(1)}, u32[]{:S(2)}, u32[]{:S(2)}) %collective-permute-start.43) | collective-permute-done | bytes 786464 | tf_op jit(solution)/shard_map/ppermute | solution.py:343
  554.2 5.5 collective-permute-done.44
  563.5 7.6 %collective-permute-done.45 = bf16[48,2048]{1,0:T(8,128)(2,1)S(1)} collective-permute-done((bf16[48,2048]{1,0:T(8,128)(2,1)S(1)}, bf16[48,2048]{1,0:T(8,128)(2,1)S(1)}, u32[]{:S(2)}, u32[]{:S(2)}) %collective-permute-start.45) | collective-permute-done | bytes 196640 | tf_op jit(solution)/shard_map/ppermute | solution.py:343
  571.6 9.9 %collective-permute-done.46 = bf16[48,2048]{1,0:T(8,128)(2,1)S(1)} collective-permute-done((bf16[48,2048]{1,0:T(8,128)(2,1)S(1)}, bf16[48,2048]{1,0:T(8,128)(2,1)S(1)}, u32[]{:S(2)}, u32[]{:S(2)}) %collective-permute-start.46) | collective-permute-done | bytes 196640 | tf_op jit(solution)/shard_map/ppermute | solution.py:343
  584.3 5.5 reorder.3
  613.8 6.0 reorder.2
  (556 shorter events, 212.1 us)
Async XLA Ops:
  8.2 68.7 %collective-permute-start.3 = (bf16[384,1536]{1,0:T(8,128)(2,1)}, bf16[384,1536]{1,0:T(8,128)(2,1)}, u32[]{:S(2)}, u32[]{:S(2)}) collective-permute-start(bf16[384,1536]{1,0:T(8,128)(2,1)} %w0.3), channel_id=1, source_target_pairs={{0,1},{1,0},{2,3},{3,2},{4,5},{5,4},{6,7},{7,6},{8,9},{9,8},{10,11... | collective-permute-start | bytes 3538952 | tf_op jit(solution)/shard_map/ppermute | solution.py:343
  8.7 62.4 %collective-permute-start.4 = (bf16[384,1536]{1,0:T(8,128)(2,1)}, bf16[384,1536]{1,0:T(8,128)(2,1)}, u32[]{:S(2)}, u32[]{:S(2)}) collective-permute-start(bf16[384,1536]{1,0:T(8,128)(2,1)} %w0.3), channel_id=1, source_target_pairs={{0,2},{1,3},{2,0},{3,1},{4,6},{5,7},{6,4},{7,5},{8,10},{9,11},{10,... | collective-permute-start | bytes 3538952 | tf_op jit(solution)/shard_map/ppermute | solution.py:343
  8.7 62.4 %collective-permute-start.10 = (bf16[384,1536]{1,0:T(8,128)(2,1)}, bf16[384,1536]{1,0:T(8,128)(2,1)}, u32[]{:S(2)}, u32[]{:S(2)}) collective-permute-start(bf16[384,1536]{1,0:T(8,128)(2,1)} %out0.1), channel_id=1, source_target_pairs={{0,2},{1,3},{2,0},{3,1},{4,6},{5,7},{6,4},{7,5},{8,10},{9,11},{10,... | collective-permute-start | bytes 3538952 | tf_op jit(solution)/shard_map/ppermute | solution.py:343
  35.1 40.7 %collective-permute-start.6 = (bf16[256,512]{1,0:T(8,128)(2,1)S(1)}, bf16[256,512]{1,0:T(8,128)(2,1)S(1)}, u32[]{:S(2)}, u32[]{:S(2)}) collective-permute-start(bf16[256,512]{1,0:T(8,128)(2,1)S(1)} %pad_maximum_fusion.9), channel_id=1, source_target_pairs={{0,2},{1,3},{2,0},{3,1},{4,6},{5,7},{6,4},{7,5},{8,10},{9,11},{10,... | collective-permute-start | bytes 786440 | tf_op jit(solution)/shard_map/ppermute | solution.py:343
  46.5 34.8 %collective-permute-start.9 = (bf16[384,1536]{1,0:T(8,128)(2,1)S(1)}, bf16[384,1536]{1,0:T(8,128)(2,1)S(1)}, u32[]{:S(2)}, u32[]{:S(2)}) collective-permute-start(bf16[384,1536]{1,0:T(8,128)(2,1)S(1)} %copy-done.104), channel_id=1, source_target_pairs={{0,1},{1,0},{2,3},{3,2},{4,5},{5,4},{6,7},{7,6},{8,9},{9,8},{10,11... | collective-permute-start | bytes 3538952 | tf_op jit(solution)/shard_map/ppermute | solution.py:343
  78.7 52.3 %collective-permute-start.14 = (bf16[768,768]{1,0:T(8,128)(2,1)S(1)}, bf16[768,768]{1,0:T(8,128)(2,1)S(1)}, u32[]{:S(2)}, u32[]{:S(2)}) collective-permute-start(bf16[768,768]{1,0:T(8,128)(2,1)S(1)} %copy-done.101), channel_id=1, source_target_pairs={{0,4},{1,5},{2,6},{3,7},{4,0},{5,1},{6,2},{7,3},{8,12},{9,13},{10,... | collective-permute-start | bytes 3538952 | tf_op jit(solution)/shard_map/ppermute | solution.py:343
  79.0 76.9 %collective-permute-start.16 = (bf16[384,1536]{1,0:T(8,128)(2,1)S(1)}, bf16[384,1536]{1,0:T(8,128)(2,1)S(1)}, u32[]{:S(2)}, u32[]{:S(2)}) collective-permute-start(bf16[384,1536]{1,0:T(8,128)(2,1)S(1)} %copy-done.102), channel_id=1, source_target_pairs={{0,4},{1,5},{2,6},{3,7},{4,0},{5,1},{6,2},{7,3},{8,12},{9,13},{10,... | collective-permute-start | bytes 3538952 | tf_op jit(solution)/shard_map/ppermute | solution.py:343
  81.3 74.6 %collective-permute-start.22 = (bf16[256,1664]{1,0:T(8,128)(2,1)S(1)}, bf16[256,1664]{1,0:T(8,128)(2,1)S(1)}, u32[]{:S(2)}, u32[]{:S(2)}) collective-permute-start(bf16[256,1664]{1,0:T(8,128)(2,1)S(1)} %copy-done.14), channel_id=1, source_target_pairs={{0,8},{1,9},{2,10},{3,11},{4,12},{5,13},{6,14},{7,15},{8,16},{9,17... | collective-permute-start | bytes 2555912 | tf_op jit(solution)/shard_map/ppermute | solution.py:352
  83.0 76.1 %collective-permute-start.11 = (bf16[384,1536]{1,0:T(8,128)(2,1)}, bf16[384,1536]{1,0:T(8,128)(2,1)S(1)}, u32[]{:S(2)}, u32[]{:S(2)}) collective-permute-start(bf16[384,1536]{1,0:T(8,128)(2,1)} %collective-permute-done.10.out2), channel_id=1, source_target_pairs={{0,1},{1,0},{2,3},{3,2},{4,5},{5,4},{6,7},{7,6},{8,9},{9,8},{10,11... | collective-permute-start | bytes 3538952 | tf_op jit(solution)/shard_map/ppermute | solution.py:343
  105.7 58.0 %collective-permute-start.13 = (bf16[768,768]{1,0:T(8,128)(2,1)S(1)}, bf16[768,768]{1,0:T(8,128)(2,1)S(1)}, u32[]{:S(2)}, u32[]{:S(2)}) collective-permute-start(bf16[768,768]{1,0:T(8,128)(2,1)S(1)} %collective-permute-done.12), channel_id=1, source_target_pairs={{0,1},{1,0},{2,3},{3,2},{4,5},{5,4},{6,7},{7,6},{8,9},{9,8},{10,11... | collective-permute-start | bytes 3538952 | tf_op jit(solution)/shard_map/ppermute | solution.py:343
  131.0 34.4 %collective-permute-start.15 = (bf16[768,768]{1,0:T(8,128)(2,1)S(1)}, bf16[768,768]{1,0:T(8,128)(2,1)S(1)}, u32[]{:S(2)}, u32[]{:S(2)}) collective-permute-start(bf16[768,768]{1,0:T(8,128)(2,1)S(1)} %collective-permute-done.14), channel_id=1, source_target_pairs={{0,1},{1,0},{2,3},{3,2},{4,5},{5,4},{6,7},{7,6},{8,9},{9,8},{10,11... | collective-permute-start | bytes 3538952 | tf_op jit(solution)/shard_map/ppermute | solution.py:343
  155.9 99.2 %collective-permute-start.23 = (bf16[256,1664]{1,0:T(8,128)(2,1)S(1)}, bf16[256,1664]{1,0:T(8,128)(2,1)S(1)}, u32[]{:S(2)}, u32[]{:S(2)}) collective-permute-start(bf16[256,1664]{1,0:T(8,128)(2,1)S(1)} %collective-permute-done.22.dy_ref.refs_6_), channel_id=1, source_target_pairs={{0,8},{1,9},{2,10},{3,11},{4,12},{5,13},{6,14},{7,15},{8,16},{9,17... | collective-permute-start | bytes 2555912 | tf_op jit(solution)/shard_map/ppermute | solution.py:352
  162.0 34.3 %collective-permute-start.18 = (bf16[256,1536]{1,0:T(8,128)(2,1)S(1)}, bf16[256,1536]{1,0:T(8,128)(2,1)S(1)}, u32[]{:S(2)}, u32[]{:S(2)}) collective-permute-start(bf16[256,1536]{1,0:T(8,128)(2,1)S(1)} %multiply_convert_fusion.h2_ref.refs_0_), channel_id=1, source_target_pairs={{0,8},{1,9},{2,10},{3,11},{4,12},{5,13},{6,14},{7,15},{8,16},{9,17... | collective-permute-start | bytes 2359304 | tf_op jit(solution)/shard_map/ppermute | solution.py:352
  214.2 181.1 %collective-permute-start.49 = (bf16[256,384]{1,0:T(8,128)(2,1)}, bf16[256,384]{1,0:T(8,128)(2,1)}, u32[]{:S(2)}, u32[]{:S(2)}) collective-permute-start(bf16[256,384]{1,0:T(8,128)(2,1)} %get-tuple-element.105), channel_id=1, source_target_pairs={{0,1},{1,0},{2,3},{3,2},{4,5},{5,4},{6,7},{7,6},{8,9},{9,8},{10,11... | collective-permute-start | bytes 589832 | tf_op jit(solution)/shard_map/ppermute | solution.py:343
  214.2 39.4 %collective-permute-start.24 = (bf16[256,1536]{1,0:T(8,128)(2,1)S(1)}, bf16[256,1536]{1,0:T(8,128)(2,1)}, u32[]{:S(2)}, u32[]{:S(2)}) collective-permute-start(bf16[256,1536]{1,0:T(8,128)(2,1)S(1)} %get-tuple-element.47), channel_id=1, source_target_pairs={{0,8},{1,9},{2,10},{3,11},{4,12},{5,13},{6,14},{7,15},{8,16},{9,17... | collective-permute-start | bytes 2359304 | tf_op jit(solution)/shard_map/ppermute | solution.py:352
  233.4 36.9 %collective-permute-start.20 = (bf16[256,1536]{1,0:T(8,128)(2,1)S(1)}, bf16[256,1536]{1,0:T(8,128)(2,1)S(1)}, u32[]{:S(2)}, u32[]{:S(2)}) collective-permute-start(bf16[256,1536]{1,0:T(8,128)(2,1)S(1)} %collective-permute-done.19.h2_ref.refs_2_), channel_id=1, source_target_pairs={{0,8},{1,9},{2,10},{3,11},{4,12},{5,13},{6,14},{7,15},{8,16},{9,17... | collective-permute-start | bytes 2359304 | tf_op jit(solution)/shard_map/ppermute | solution.py:352
  238.2 50.5 %collective-permute-start.28 = (bf16[256,1664]{1,0:T(8,128)(2,1)S(1)}, bf16[256,1664]{1,0:T(8,128)(2,1)S(1)}, u32[]{:S(2)}, u32[]{:S(2)}) collective-permute-start(bf16[256,1664]{1,0:T(8,128)(2,1)S(1)} %add_convert_fusion.10), channel_id=1, source_target_pairs={{0,8},{1,9},{2,10},{3,11},{4,12},{5,13},{6,14},{7,15},{8,16},{9,17... | collective-permute-start | bytes 2555912 | tf_op jit(solution)/shard_map/ppermute | solution.py:352
  255.0 50.6 %collective-permute-start.25 = (bf16[256,1536]{1,0:T(8,128)(2,1)S(1)}, bf16[256,1536]{1,0:T(8,128)(2,1)}, u32[]{:S(2)}, u32[]{:S(2)}) collective-permute-start(bf16[256,1536]{1,0:T(8,128)(2,1)S(1)} %add_convert_fusion.13), channel_id=1, source_target_pairs={{0,8},{1,9},{2,10},{3,11},{4,12},{5,13},{6,14},{7,15},{8,16},{9,17... | collective-permute-start | bytes 2359304 | tf_op jit(solution)/shard_map/ppermute | solution.py:352
  288.9 34.9 %collective-permute-start.29 = (bf16[256,1664]{1,0:T(8,128)(2,1)S(1)}, bf16[256,1664]{1,0:T(8,128)(2,1)S(1)}, u32[]{:S(2)}, u32[]{:S(2)}) collective-permute-start(bf16[256,1664]{1,0:T(8,128)(2,1)S(1)} %add_convert_fusion.9), channel_id=1, source_target_pairs={{0,8},{1,9},{2,10},{3,11},{4,12},{5,13},{6,14},{7,15},{8,16},{9,17... | collective-permute-start | bytes 2555912 | tf_op jit(solution)/shard_map/ppermute | solution.py:352
  307.8 109.4 %collective-permute-start.26 = (bf16[256,1536]{1,0:T(8,128)(2,1)}, bf16[256,1536]{1,0:T(8,128)(2,1)}, u32[]{:S(2)}, u32[]{:S(2)}) collective-permute-start(bf16[256,1536]{1,0:T(8,128)(2,1)} %add_convert_fusion.12), channel_id=1, source_target_pairs={{0,8},{1,9},{2,10},{3,11},{4,12},{5,13},{6,14},{7,15},{8,16},{9,17... | collective-permute-start | bytes 2359304 | tf_op jit(solution)/shard_map/ppermute | solution.py:352
  316.4 116.0 %collective-permute-start.61 = (bf16[768,1536]{1,0:T(8,128)(2,1)}, bf16[768,1536]{1,0:T(8,128)(2,1)}, u32[]{:S(2)}, u32[]{:S(2)}) collective-permute-start(bf16[768,1536]{1,0:T(8,128)(2,1)} %get-tuple-element.67), channel_id=1, source_target_pairs={{0,1},{1,0},{2,3},{3,2},{4,5},{5,4},{6,7},{7,6},{8,9},{9,8},{10,11... | collective-permute-start | bytes 7077896 | tf_op jit(solution)/shard_map/ppermute | solution.py:343
  352.5 83.2 %collective-permute-start.69 = (bf16[768,1536]{1,0:T(8,128)(2,1)}, bf16[768,1536]{1,0:T(8,128)(2,1)}, u32[]{:S(2)}, u32[]{:S(2)}) collective-permute-start(bf16[768,1536]{1,0:T(8,128)(2,1)} %expert_down_grads.3), channel_id=1, source_target_pairs={{0,1},{1,0},{2,3},{3,2},{4,5},{5,4},{6,7},{7,6},{8,9},{9,8},{10,11... | collective-permute-start | bytes 7077896 | tf_op jit(solution)/shard_map/ppermute | solution.py:343
  428.4 48.8 %collective-permute-start.37 = (bf16[256,384]{1,0:T(8,128)(2,1)}, bf16[256,384]{1,0:T(8,128)(2,1)S(1)}, u32[]{:S(2)}, u32[]{:S(2)}) collective-permute-start(bf16[256,384]{1,0:T(8,128)(2,1)} %get-tuple-element.109), channel_id=1, source_target_pairs={{0,1},{1,0},{2,3},{3,2},{4,5},{5,4},{6,7},{7,6},{8,9},{9,8},{10,11... | collective-permute-start | bytes 589832 | tf_op jit(solution)/shard_map/ppermute | solution.py:343
  428.4 50.4 %collective-permute-start.38 = (bf16[256,384]{1,0:T(8,128)(2,1)}, bf16[256,384]{1,0:T(8,128)(2,1)S(1)}, u32[]{:S(2)}, u32[]{:S(2)}) collective-permute-start(bf16[256,384]{1,0:T(8,128)(2,1)} %get-tuple-element.108), channel_id=1, source_target_pairs={{0,2},{1,3},{2,0},{3,1},{4,6},{5,7},{6,4},{7,5},{8,10},{9,11},{10,... | collective-permute-start | bytes 589832 | tf_op jit(solution)/shard_map/ppermute | solution.py:343
  478.8 70.5 %collective-permute-start.70 = (bf16[384,1536]{1,0:T(8,128)(2,1)S(1)}, bf16[384,1536]{1,0:T(8,128)(2,1)S(1)}, u32[]{:S(2)}, u32[]{:S(2)}) collective-permute-start(bf16[384,1536]{1,0:T(8,128)(2,1)S(1)} %add_convert_fusion.2), channel_id=1, source_target_pairs={{0,4},{1,5},{2,6},{3,7},{4,0},{5,1},{6,2},{7,3},{8,12},{9,13},{10,... | collective-permute-start | bytes 3538952 | tf_op jit(solution)/shard_map/ppermute | solution.py:343
  484.4 77.4 %collective-permute-start.63 = (bf16[768,768]{1,0:T(8,128)(2,1)S(1)}, bf16[768,768]{1,0:T(8,128)(2,1)}, u32[]{:S(2)}, u32[]{:S(2)}) collective-permute-start(bf16[768,768]{1,0:T(8,128)(2,1)S(1)} %add_convert_fusion.7), channel_id=1, source_target_pairs={{0,2},{1,3},{2,0},{3,1},{4,6},{5,7},{6,4},{7,5},{8,10},{9,11},{10,... | collective-permute-start | bytes 3538952 | tf_op jit(solution)/shard_map/ppermute | solution.py:343
  489.3 59.0 %collective-permute-start.43 = (bf16[4,48,2048]{2,1,0:T(8,128)(2,1)S(1)}, bf16[4,48,2048]{2,1,0:T(8,128)(2,1)S(1)}, u32[]{:S(2)}, u32[]{:S(2)}) collective-permute-start(bf16[4,48,2048]{2,1,0:T(8,128)(2,1)S(1)} %slice_bitcast_fusion), channel_id=1, source_target_pairs={{0,4},{1,5},{2,6},{3,7},{4,0},{5,1},{6,2},{7,3},{8,12},{9,13},{10,... | collective-permute-start | bytes 2359304 | tf_op jit(solution)/shard_map/ppermute | solution.py:343
  508.5 62.7 %collective-permute-start.67 = (bf16[768,768]{1,0:T(8,128)(2,1)S(1)}, bf16[768,768]{1,0:T(8,128)(2,1)S(1)}, u32[]{:S(2)}, u32[]{:S(2)}) collective-permute-start(bf16[768,768]{1,0:T(8,128)(2,1)S(1)} %add_convert_fusion.4), channel_id=1, source_target_pairs={{0,2},{1,3},{2,0},{3,1},{4,6},{5,7},{6,4},{7,5},{8,10},{9,11},{10,... | collective-permute-start | bytes 3538952 | tf_op jit(solution)/shard_map/ppermute | solution.py:343
  509.0 43.6 %collective-permute-start.59 = (bf16[2,48,1536]{2,1,0:T(8,128)(2,1)S(1)}, bf16[2,48,1536]{2,1,0:T(8,128)(2,1)S(1)}, u32[]{:S(2)}, u32[]{:S(2)}) collective-permute-start(bf16[2,48,1536]{2,1,0:T(8,128)(2,1)S(1)} %get-tuple-element.120), channel_id=1, source_target_pairs={{0,8},{1,9},{2,10},{3,11},{4,12},{5,13},{6,14},{7,15},{8,0},{9,1},... | collective-permute-start | bytes 884744 | tf_op jit(solution)/shard_map/ppermute | solution.py:343
  551.0 31.4 %collective-permute-start.71 = (bf16[384,1536]{1,0:T(8,128)(2,1)S(1)}, bf16[384,1536]{1,0:T(8,128)(2,1)S(1)}, u32[]{:S(2)}, u32[]{:S(2)}) collective-permute-start(bf16[384,1536]{1,0:T(8,128)(2,1)S(1)} %add_convert_fusion.1), channel_id=1, source_target_pairs={{0,2},{1,3},{2,0},{3,1},{4,6},{5,7},{6,4},{7,5},{8,10},{9,11},{10,... | collective-permute-start | bytes 3538952 | tf_op jit(solution)/shard_map/ppermute | solution.py:343
  552.7 31.7 %collective-permute-start.60 = (bf16[4,48,1536]{2,1,0:T(8,128)(2,1)S(1)}, bf16[4,48,1536]{2,1,0:T(8,128)(2,1)}, u32[]{:S(2)}, u32[]{:S(2)}) collective-permute-start(bf16[4,48,1536]{2,1,0:T(8,128)(2,1)S(1)} %bitcast.167), channel_id=1, source_target_pairs={{0,4},{1,5},{2,6},{3,7},{4,0},{5,1},{6,2},{7,3},{8,12},{9,13},{10,... | collective-permute-start | bytes 1769480 | tf_op jit(solution)/shard_map/ppermute | solution.py:343
  563.4 33.2 %collective-permute-start.64 = (bf16[768,768]{1,0:T(8,128)(2,1)S(1)}, bf16[768,768]{1,0:T(8,128)(2,1)}, u32[]{:S(2)}, u32[]{:S(2)}) collective-permute-start(bf16[768,768]{1,0:T(8,128)(2,1)S(1)} %add_convert_fusion.6), channel_id=1, source_target_pairs={{0,1},{1,0},{2,3},{3,2},{4,5},{5,4},{6,7},{7,6},{8,9},{9,8},{10,11... | collective-permute-start | bytes 3538952 | tf_op jit(solution)/shard_map/ppermute | solution.py:343
  (183 other events, 2291.2 us)

commit v2 on v1

--- a/solution.py
+++ b/solution.py
@@ -334,6 +334,10 @@
 F32 = jnp.float32
 
 
+def cost(microseconds):
+    return pl.CostEstimate(flops=microseconds * 10**9, bytes_accessed=10**5, transcendentals=0)
+
+
 def swap(values, expert_bits, shard_bits):
     pairs = [
         (e * N_SHARD + s, (e ^ expert_bits) * N_SHARD + (s ^ shard_bits))
@@ -363,6 +367,14 @@
     high = (index & 2) == 2
     once = [jnp.where(odd, blocks[j ^ 1], blocks[j]) for j in range(4)]
     return [jnp.where(high, once[j ^ 2], once[j]) for j in range(4)]
+
+
+def together(*values):
+    return lax.optimization_barrier(values)
+
+
+def after(value, *others):
+    return lax.optimization_barrier((value,) + others)[0]
 
 
 def rejoin(mine, partner, low_first):
@@ -449,8 +461,8 @@
             jax.ShapeDtypeStruct((HQ, rows, seq_len), BF16),
             jax.ShapeDtypeStruct((rows, width), BF16),
         ],
-        compiler_params=pltpu.CompilerParams(vmem_limit_bytes=40 * MEBIBYTE),
-        cost_estimate=pl.CostEstimate(flops=5 * 10**9, bytes_accessed=2 * 10**7, transcendentals=3 * 10**6),
+        compiler_params=pltpu.CompilerParams(vmem_limit_bytes=56 * MEBIBYTE),
+        cost_estimate=cost(15),
         name="attention_forward",
     )(where, h1_rel, *w_query, keys_values, keys_values, cosine, sine, seg_query, seg_key)
 
@@ -548,25 +560,30 @@
             jax.ShapeDtypeStruct((seq_len, KVH * HEAD), BF16),
             jax.ShapeDtypeStruct((rows, width), F32),
         ],
-        compiler_params=pltpu.CompilerParams(vmem_limit_bytes=48 * MEBIBYTE),
-        cost_estimate=pl.CostEstimate(flops=8 * 10**9, bytes_accessed=3 * 10**7, transcendentals=0),
+        compiler_params=pltpu.CompilerParams(vmem_limit_bytes=56 * MEBIBYTE),
+        cost_estimate=cost(17),
         name="attention_backward",
     )(where, branch, *w_out, attended, queries, probs, keys_values, keys_values, *w_query, cosine, sine)
 
 
 def expert_body(
-    where_ref, h2_ref, dy_ref, router_ref, gate_own, up_own, down_own, gate_far, up_far, down_far,
-    message_out, mixed_out, da_out, db_out, act_out, gates_ref, dh_acc, y_acc, gg_acc,
+    where_ref, h2_ref, dy_ref, router_ref, *refs,
 ):
+    own, far = refs[:6], refs[6:12]
+    message_out, mixed_out, da_out, db_out, act_out, gates_ref, dh_acc, y_acc, gg_acc = refs[12:]
     e = pl.program_id(0)
     f = pl.program_id(1)
     rows, width = h2_ref.shape
+    half = width // 2
     lane = lax.broadcasted_iota(jnp.int32, (rows, LANES), 1)
+    places = [pl.ds(pl.multiple_of((where_ref[1] ^ i) * half, LANES), half) for i in range(2)]
 
     @pl.when((e == 0) & (f == 0))
     def _():
         named = dy_ref[:, width:].astype(F32) > 0.5
-        logits = jnp.where(named, dot_nn(h2_ref[...], router_ref[...]), MASKED_SCORE)
+        logits = dot_nt(h2_ref[...], router_ref[...])
+        logits = jnp.concatenate([logits, jnp.zeros((rows, LANES - logits.shape[1]), F32)], 1)
+        logits = jnp.where(named, logits, MASKED_SCORE)
         top = jnp.max(logits, -1, keepdims=True)
         weights = jnp.where(named, jnp.exp(logits - top), 0.0)
         gates_ref[...] = weights / jnp.sum(weights, -1, keepdims=True)
@@ -576,12 +593,15 @@
 
     here = lane == (where_ref[0] ^ e)
 
-    def work(gate_ref, up_ref, down_ref):
+    def work(members):
+        gates, ups, downs = [[members[2 * k + i] for i in range(2)] for k in range(3)]
         gate = jnp.sum(jnp.where(here, gates_ref[...], 0.0), -1, keepdims=True)
-        h2 = h2_ref[...]
-        a = dot_nn(h2, gate_ref[...])
-        b = dot_nn(h2, up_ref[...])
-        d_plain = dot_nt(dy_ref[:, :width], down_ref[...])
+        h2 = [h2_ref[:, place] for place in places]
+        dy = [dy_ref[:, place] for place in places]
+        load = lambda ref: ref[...].reshape(ref.shape[-2:])
+        a = dot_nn(h2[0], load(gates[0])) + dot_nn(h2[1], load(gates[1]))
+        b = dot_nn(h2[0], load(ups[0])) + dot_nn(h2[1], load(ups[1]))
+        d_plain = dot_nt(dy[0], load(downs[0])) + dot_nt(dy[1], load(downs[1]))
         sigmoid = 1.0 / (1.0 + jnp.exp(-a))
         silu = a * sigmoid
         act = silu * b
@@ -594,29 +614,32 @@
         da_out[...] = d_a
         db_out[...] = d_b
         act_out[...] = scaled
-        dh_acc[...] += dot_nt(d_a, gate_ref[...]) + dot_nt(d_b, up_ref[...])
-        y_acc[...] += dot_nn(scaled, down_ref[...])
+        for i in range(2):
+            dh_acc[i] += dot_nt(d_a, load(gates[i])) + dot_nt(d_b, load(ups[i]))
+            y_acc[i] += dot_nn(scaled, load(downs[i]))
 
     @pl.when(e == 0)
     def _():
-        work(gate_own, up_own, down_own)
+        work(own)
 
     @pl.when(e == 1)
     def _():
-        work(gate_far, up_far, down_far)
+        work(far)
 
     @pl.when((e == pl.num_programs(0) - 1) & (f == pl.num_programs(1) - 1))
     def _():
-        message_out[:, :width] = dh_acc[...].astype(BF16)
+        for i in range(2):
+            message_out[:, places[i]] = dh_acc[i].astype(BF16)
+            mixed_out[:, places[i]] = y_acc[i].astype(BF16)
         high = gg_acc[...].astype(BF16).astype(F32)
         low = pltpu.roll(gg_acc[...] - high, N_EXPERT, 1)
         message_out[:, width:] = (high + low).astype(BF16)
-        mixed_out[...] = y_acc[...].astype(BF16)
 
 
 def expert_block(where, h2, dy_routes, router, own, far):
     rows, width = h2.shape
     hidden = own[0].shape[1]
+    half = width // 2
     chunk = 256
     chunks = hidden // chunk
 
@@ -625,25 +648,24 @@
 
     own_step = lambda e, f: jnp.where(e == 0, f, chunks - 1)
     far_step = lambda e, f: jnp.where(e == 0, 0, f)
-    own_in = pl.BlockSpec((width, chunk), lambda e, f, w: (0, own_step(e, f)))
-    own_down = pl.BlockSpec((chunk, width), lambda e, f, w: (own_step(e, f), 0))
-    far_in = pl.BlockSpec((width, chunk), lambda e, f, w: (0, far_step(e, f)))
-    far_down = pl.BlockSpec((chunk, width), lambda e, f, w: (far_step(e, f), 0))
+    own_in = [pl.BlockSpec((half, chunk), lambda e, f, w, i=i: (w[1] ^ i, own_step(e, f))) for i in range(2)]
+    own_down = [pl.BlockSpec((chunk, half), lambda e, f, w, i=i: (own_step(e, f), w[1] ^ i)) for i in range(2)]
+    far_in = [pl.BlockSpec((1, half, chunk), lambda e, f, w, k=k: (k, 0, far_step(e, f))) for k in range(2)]
+    far_down = pl.BlockSpec((1, chunk, half), lambda e, f, w: (2, far_step(e, f), 0))
     part = pl.BlockSpec((rows, chunk), lambda e, f, w: (0, e * chunks + f))
     return pl.pallas_call(
         expert_body,
         grid_spec=pltpu.PrefetchScalarGridSpec(
             num_scalar_prefetch=1,
             grid=(2, chunks),
-            in_specs=[
-                whole((rows, width)), whole(dy_routes.shape), whole(router.shape),
-                own_in, own_in, own_down, far_in, far_in, far_down,
-            ],
+            in_specs=[whole((rows, width)), whole(dy_routes.shape), whole(router.shape)]
+            + own_in + own_in + own_down
+            + [far_in[0], far_in[0], far_in[1], far_in[1], far_down, far_down],
             out_specs=[whole((rows, width + LANES)), whole((rows, width)), part, part, part],
             scratch_shapes=[
                 pltpu.VMEM((rows, LANES), F32),
-                pltpu.VMEM((rows, width), F32),
-                pltpu.VMEM((rows, width), F32),
+                pltpu.VMEM((2, rows, half), F32),
+                pltpu.VMEM((2, rows, half), F32),
                 pltpu.VMEM((rows, LANES), F32),
             ],
         ),
@@ -654,10 +676,13 @@
             jax.ShapeDtypeStruct((rows, 2 * hidden), BF16),
             jax.ShapeDtypeStruct((rows, 2 * hidden), BF16),
         ],
-        compiler_params=pltpu.CompilerParams(vmem_limit_bytes=40 * MEBIBYTE),
-        cost_estimate=pl.CostEstimate(flops=8 * 10**9, bytes_accessed=2 * 10**7, transcendentals=4 * 10**5),
+        compiler_params=pltpu.CompilerParams(vmem_limit_bytes=28 * MEBIBYTE),
+        cost_estimate=cost(20),
         name="expert_block",
-    )(where, h2, dy_routes, router, *own, *far)
+    )(
+        where, h2, dy_routes, router, own[0], own[0], own[1], own[1], own[2], own[2],
+        far[0], far[1], far[0], far[1], far[0], far[1],
+    )
 
 
 def summed_products_body(where_ref, *refs, parts, sets):
@@ -690,68 +715,288 @@
             out_specs=[out_spec] * sets,
         ),
         out_shape=[jax.ShapeDtypeStruct(out_shape, BF16)] * sets,
-        compiler_params=pltpu.CompilerParams(vmem_limit_bytes=48 * MEBIBYTE),
-        cost_estimate=pl.CostEstimate(flops=3 * 10**9, bytes_accessed=10**7, transcendentals=0),
+        compiler_params=pltpu.CompilerParams(vmem_limit_bytes=56 * MEBIBYTE),
+        cost_estimate=cost(5),
         name=name,
     )(where, *lefts, *[member for members in right_sets for member in members])
 
 
-def sum_over_planes(pieces):
-    shape = pieces.shape[1:]
-    low = pieces.reshape((4, 2) + shape)
-    kept = low[:, 0].astype(F32) + swap(low[:, 1], 1, 0).astype(F32)
-    kept = kept.astype(BF16).reshape((2, 2) + shape)
-    kept = kept[:, 0].astype(F32) + swap(kept[:, 1], 2, 0).astype(F32)
-    kept = kept.astype(BF16)
-    own = (kept[0].astype(F32) + swap(kept[1], 4, 0).astype(F32)).astype(BF16)
-    two = jnp.stack([own, swap(own, 4, 0)])
-    four = jnp.stack([two, swap(two, 2, 0)], 1).reshape((4,) + shape)
-    return four, swap(four, 1, 0)
-
-
-def reorder_body(where_ref, even_ref, odd_ref, out_ref):
-    place = where_ref[0] ^ pl.program_id(0)
-
-    @pl.when(place % 2 == 0)
+def in_grads_body(where_ref, *refs):
+    h2_refs, da_refs, db_refs = refs[:4], refs[4:8], refs[8:12]
+    send_ref, keep_ref, turned_ref = refs[12:]
+    rows = h2_refs[0].shape[0]
+    half = turned_ref.shape[0] // 2
+
+    @pl.when(pl.program_id(0) == 0)
     def _():
-        out_ref[...] = even_ref[...].astype(F32)
-
-    @pl.when(place % 2 == 1)
-    def _():
-        out_ref[...] = odd_ref[...].astype(F32)
-
-
-def reorder(where, even, odd):
-    shape = even.shape[1:]
-    spec = pl.BlockSpec((1,) + shape, lambda b, w: ((w[0] ^ b) // 2, 0, 0))
+        for j in range(4):
+            turned_ref[:, j * rows : (j + 1) * rows] = h2_refs[j][...].T
+
+    for k, member in enumerate((da_refs, db_refs)):
+        for out, place in ((send_ref, 1 - where_ref[0]), (keep_ref, where_ref[0])):
+            here = pl.ds(pl.multiple_of(place * half, LANES), half)
+            total = dot_nn(turned_ref[here, :rows], member[0][...])
+            for j in range(1, 4):
+                total = total + dot_nn(turned_ref[here, j * rows : (j + 1) * rows], member[j][...])
+            out[k] = total.astype(BF16)
+
+
+def expert_in_grads(where, h2, d_a, d_b):
+    rows, width = h2[0].shape
+    columns = d_a[0].shape[1]
+    chunk = 256
+    half = width // 2
+    part = pl.BlockSpec((rows, chunk), lambda i, w: (0, i))
+    out = pl.BlockSpec((2, half, chunk), lambda i, w: (0, 0, i))
     return pl.pallas_call(
-        reorder_body,
+        in_grads_body,
         grid_spec=pltpu.PrefetchScalarGridSpec(
             num_scalar_prefetch=1,
-            grid=(N_EXPERT,),
-            in_specs=[spec, spec],
-            out_specs=pl.BlockSpec((1,) + shape, lambda b, w: (b, 0, 0)),
+            grid=(columns // chunk,),
+            in_specs=[pl.BlockSpec((rows, width), lambda i, w: (0, 0))] * 4 + [part] * 8,
+            out_specs=[out] * 2,
+            scratch_shapes=[pltpu.VMEM((width, 4 * rows), BF16)],
         ),
-        out_shape=jax.ShapeDtypeStruct((N_EXPERT,) + shape, F32),
-        name="reorder",
-    )(where, even, odd).reshape(N_EXPERT * shape[0], shape[1])
-
-
-def fetch_far(mine, core):
-    half = mine.shape[0] // 2
-    part = swap(lax.dynamic_slice_in_dim(mine, core * half, half, 0), 1, 0)
-    return rejoin(part, swap(part, 0, 1), core == 0)
-
-
-def expert_weight_sums(send, keep, axis, core):
-    received = swap(send, 0, 1)
-    half = send.shape[axis] // 2
-    cut = lambda a, i: lax.slice_in_dim(a, i * half, (i + 1) * half, axis=axis).astype(F32)
-    for_far = (cut(keep, 1) + cut(received, 1)).astype(BF16)
-    total = cut(keep, 0) + cut(received, 0) + swap(for_far, 1, 0).astype(F32)
-    total = total.astype(BF16)
-    total = (total.astype(F32) + swap(total, 0, 2).astype(F32)).astype(BF16)
-    return rejoin(total, swap(total, 0, 1), core == 0).astype(F32)[None]
+        out_shape=[jax.ShapeDtypeStruct((2, half, columns), BF16)] * 2,
+        compiler_params=pltpu.CompilerParams(vmem_limit_bytes=30 * MEBIBYTE),
+        cost_estimate=cost(1),
+        name="expert_in_grads",
+    )(where, *h2, *d_a, *d_b)
+
+
+def down_grads_body(where_ref, *refs):
+    send_refs, keep_refs, dy_refs = refs[:4], refs[4:8], refs[8:12]
+    for lefts, out in ((send_refs, refs[12]), (keep_refs, refs[13])):
+        total = dot_tn(lefts[0][...], dy_refs[0][...])
+        for j in range(1, 4):
+            total = total + dot_tn(lefts[j][...], dy_refs[j][...])
+        out[...] = total.astype(BF16)
+
+
+def expert_down_grads(where, acts, dy_routes):
+    rows, columns = acts[0].shape
+    width = dy_routes[0].shape[1] - LANES
+    half = columns // 4
+    out = pl.BlockSpec((half, width), lambda e, w: (e, 0))
+    return pl.pallas_call(
+        down_grads_body,
+        grid_spec=pltpu.PrefetchScalarGridSpec(
+            num_scalar_prefetch=1,
+            grid=(2,),
+            in_specs=[pl.BlockSpec((rows, half), lambda e, w: (0, 2 * e + 1 - w[0]))] * 4
+            + [pl.BlockSpec((rows, half), lambda e, w: (0, 2 * e + w[0]))] * 4
+            + [pl.BlockSpec((rows, width), lambda e, w: (0, 0))] * 4,
+            out_specs=[out, out],
+        ),
+        out_shape=[jax.ShapeDtypeStruct((2 * half, width), BF16)] * 2,
+        compiler_params=pltpu.CompilerParams(vmem_limit_bytes=26 * MEBIBYTE),
+        cost_estimate=cost(20),
+        name="expert_down_grads",
+    )(where, *acts, *acts, *dy_routes)
+
+
+class PlaneSum:
+    def __init__(self, pieces, order):
+        self.shape = pieces.shape[1:]
+        self.order = order
+        self.axes = [4, 2, 1]
+        self.kept = pieces.reshape((2, 2, 2) + self.shape)
+        self.step = 0
+        self.send()
+
+    def send(self):
+        if self.step < 3:
+            at = self.axes.index(self.order[self.step])
+            self.mine = lax.index_in_dim(self.kept, 0, at, keepdims=False)
+            other = lax.index_in_dim(self.kept, 1, at, keepdims=False)
+            self.received = swap(other, self.order[self.step], 0)
+        else:
+            self.received = swap(self.kept, self.order[5 - self.step], 0)
+
+    def receive(self, token):
+        received = after(self.received, token)
+        if self.step < 3:
+            self.kept = (self.mine.astype(F32) + received.astype(F32)).astype(BF16)
+            self.axes.remove(self.order[self.step])
+        else:
+            bit = self.order[5 - self.step]
+            if self.step == 5:
+                self.done = (self.kept.reshape((4,) + self.shape), received.reshape((4,) + self.shape))
+                return received
+            at = sum(1 for b in self.axes if b > bit)
+            self.kept = jnp.stack([self.kept, received], at)
+            self.axes = sorted(self.axes + [bit], reverse=True)
+        self.step += 1
+        self.send()
+        return self.kept
+
+
+def reorder_body(where_ref, even_ref, odd_ref, out_ref, *, first):
+    for b in range(N_EXPERT):
+        place = where_ref[0] ^ b
+        low = place % first
+        index = (place // (2 * first)) * first + low
+        odd = (place // first) % 2
+
+        @pl.when(odd == 0)
+        def _(b=b, index=index):
+            out_ref[b] = even_ref[index].astype(F32)
+
+        @pl.when(odd == 1)
+        def _(b=b, index=index):
+            out_ref[b] = odd_ref[index].astype(F32)
+
+
+def reorder(where, even, odd, columns, first):
+    deep, width = even.shape[1:]
+    results = []
+    begin = 0
+    for count in columns:
+        wide = min(count, 512)
+        start = begin // wide
+        spec = pl.BlockSpec((N_EXPERT // 2, deep, wide), lambda i, w, start=start: (0, 0, start + i))
+        results.append(
+            pl.pallas_call(
+                functools.partial(reorder_body, first=first),
+                grid_spec=pltpu.PrefetchScalarGridSpec(
+                    num_scalar_prefetch=1,
+                    grid=(count // wide,),
+                    in_specs=[spec, spec],
+                    out_specs=pl.BlockSpec((N_EXPERT, deep, wide), lambda i, w: (0, 0, i)),
+                ),
+                out_shape=jax.ShapeDtypeStruct((N_EXPERT, deep, count), F32),
+                cost_estimate=cost(2),
+                name="reorder",
+            )(where, even, odd).reshape(N_EXPERT * deep, count)
+        )
+        begin += count
+    return results
+
+
+def key_value_grad_body(*refs):
+    lefts, rights, out_ref = refs[:4], refs[4:8], refs[8]
+    rows, block = lefts[0].shape
+    total = dot_tn(lefts[0][...], rights[0][:rows])
+    small = rights[0][rows:, :block].astype(F32)
+    for j in range(1, 4):
+        total = total + dot_tn(lefts[j][...], rights[j][:rows])
+        small = small + rights[j][rows:, :block].astype(F32)
+    few = small.shape[0] // 2
+    out_ref[:block] = total.astype(BF16)
+    out_ref[block:, :block] = (small[:few] + small[few:]).astype(BF16)
+    out_ref[block:, block:] = jnp.zeros_like(out_ref[block:, block:])
+
+
+def key_value_grad(lefts, rights, block):
+    rows = lefts[0].shape[0]
+    columns = rights[0].shape[1]
+    few = (rights[0].shape[0] - rows) // 2
+    whole = lambda shape: pl.BlockSpec(shape, lambda i: (0, 0))
+    return pl.pallas_call(
+        key_value_grad_body,
+        grid=(1,),
+        in_specs=[whole((rows, block))] * 4 + [whole(rights[0].shape)] * 4,
+        out_specs=whole((block + few, columns)),
+        out_shape=jax.ShapeDtypeStruct((block + few, columns), BF16),
+        cost_estimate=cost(3),
+        name="key_value_grad",
+    )(*lefts, *rights)
+
+
+def place_body(where_ref, mine_ref, partner_ref, out_ref):
+    @pl.when(pl.program_id(0) == 0)
+    def _():
+        out_ref[...] = mine_ref[...].astype(out_ref.dtype)
+
+    @pl.when(pl.program_id(0) == 1)
+    def _():
+        out_ref[...] = partner_ref[...].astype(out_ref.dtype)
+
+
+def place_halves(where, mine, partner, start, half, columns, first_column, dtype):
+    wide = half // 2
+    row = start // wide
+    column = first_column // columns
+    last = half // wide - 1
+
+    def mine_map(h, i, w):
+        return (row + jnp.where(h == 0, i, last), column)
+
+    def partner_map(h, i, w):
+        return (row + jnp.where(h == 0, 0, i), column)
+
+    return pl.pallas_call(
+        place_body,
+        grid_spec=pltpu.PrefetchScalarGridSpec(
+            num_scalar_prefetch=1,
+            grid=(2, half // wide),
+            in_specs=[
+                pl.BlockSpec((wide, columns), mine_map),
+                pl.BlockSpec((wide, columns), partner_map),
+            ],
+            out_specs=pl.BlockSpec((wide, columns), lambda h, i, w: ((w[0] ^ h) * 2 + i, 0)),
+        ),
+        out_shape=jax.ShapeDtypeStruct((2 * half, columns), dtype),
+        cost_estimate=cost(3),
+        name="place_halves",
+    )(where, mine, partner)
+
+
+def far_halves_body(where_ref, *refs):
+    out_ref = refs[-1]
+    for k, ref in enumerate(refs[:-1]):
+
+        @pl.when(pl.program_id(0) == k)
+        def _(ref=ref):
+            out_ref[0] = ref[...]
+
+
+def far_halves(where, own):
+    hidden = own[0].shape[1]
+    half = own[0].shape[0] // 2
+    cuts = 2
+    tall = half // cuts
+
+    def in_map(k):
+        step = lambda i, r: jnp.where(i < k, 0, jnp.where(i == k, r, cuts - 1))
+        if k == 2:
+            return lambda i, r, w: (step(i, r), w[0])
+        return lambda i, r, w: (w[0] * cuts + step(i, r), 0)
+
+    return pl.pallas_call(
+        far_halves_body,
+        grid_spec=pltpu.PrefetchScalarGridSpec(
+            num_scalar_prefetch=1,
+            grid=(3, cuts),
+            in_specs=[pl.BlockSpec((tall, hidden), in_map(k)) for k in range(3)],
+            out_specs=pl.BlockSpec((1, tall, hidden), lambda i, r, w: (i, r, 0)),
+        ),
+        out_shape=jax.ShapeDtypeStruct((3, half, hidden), BF16),
+        cost_estimate=cost(3),
+        name="far_halves",
+    )(where, *own)
+
+
+def pack_body(key_ref, value_ref, small_ref, out_ref):
+    rows, low = key_ref.shape
+    out_ref[:rows, :low] = key_ref[...]
+    out_ref[:rows, low:] = value_ref[...]
+    out_ref[rows:, : small_ref.shape[1]] = small_ref[...]
+    out_ref[rows:, small_ref.shape[1] :] = jnp.zeros_like(out_ref[rows:, small_ref.shape[1] :])
+
+
+def pack(w_key, w_value, small):
+    rows, low = w_key.shape
+    return pl.pallas_call(
+        pack_body,
+        out_shape=jax.ShapeDtypeStruct((rows + small.shape[0], 2 * low), BF16),
+        cost_estimate=cost(2),
+        name="pack",
+    )(w_key, w_value, small)
+
+
+def plus(part, received):
+    return (part.astype(F32) + received.astype(F32)).astype(BF16)
 
 
 def on_device_rings(
@@ -770,137 +1015,173 @@
     block = width // N_SHARD
     low = KVH * HEAD
 
+    own = (expert_gate[0], expert_up[0], expert_down[0])
+    far_send = far_halves(where_core, own)
+    far_part = swap(far_send, 1, 0)
     small = jnp.concatenate(
-        [w_router, attn_gain[:, None], moe_gain[:, None], jnp.zeros((block, LANES - experts - 2), BF16)], 1
-    )
-    packed = gather_shards(jnp.concatenate([w_key, w_value, small], 1))
-    query_w = gather_shards(w_query)
-    out_w = gather_shards(w_out)
+        [w_router.T, attn_gain[None], moe_gain[None], jnp.zeros((6, block), BF16)], 0
+    )
+    packed_own = pack(after(w_key, far_send), w_value, small)
+    packed_y = swap(packed_own, 0, 2)
     mask = (routes[:, :, None] == jnp.arange(LANES, dtype=jnp.int32)[None, None, :]).any(1)
     dy_routes = [jnp.concatenate([out_grad, mask.astype(BF16)], 1)]
     for _ in range(3):
         dy_routes.append(next_plane(dy_routes[-1]))
-    own = (expert_gate[0], expert_up[0], expert_down[0])
-    far = tuple(fetch_far(member, core) for member in own)
+    query_w_core = swap(w_query, 0, 1)
+    query_w_y = swap(after(w_query, packed_y), 0, 2)
+    packed_pair = swap(jnp.concatenate([packed_own, packed_y], 0), 0, 1)
+    tall = packed_own.shape[0]
+    packed = [packed_own, packed_pair[:tall], packed_y, packed_pair[tall:]]
 
     inputs = hidden_in.astype(F32)
     factor_attn = lax.rsqrt(jnp.mean(inputs * inputs, -1, keepdims=True) + EPSILON)
     unit_rel = jnp.concatenate(
         xor_blocks([inputs[:, j * block : (j + 1) * block] for j in range(4)], shard), 1
     ) * factor_attn
-    gain_rel = jnp.concatenate([member[:, 2 * low + experts] for member in packed]).astype(F32)
-    h1_rel = (unit_rel * gain_rel).astype(BF16)
-    key_value_w = [member[:, : 2 * low] for member in packed]
+    gain_rel = jnp.concatenate([member[block + experts : block + experts + 1, :block] for member in packed], 1)
+    gain_rel = gain_rel.astype(F32)
+    h1_rel = after((unit_rel * gain_rel).astype(BF16), query_w_core)
+    key_value_w = [member[:block] for member in packed]
     pre = sum(dot_nn(h1_rel[:, j * block : (j + 1) * block], key_value_w[j]) for j in range(4))
     positions = shard * rows + jnp.arange(rows, dtype=jnp.int32)
     cosine, sine = rope_tables(positions, HEAD)
     key_local = rotate(pre[:, :low], cosine, sine, HEAD)
     key_value = jnp.concatenate([key_local, pre[:, low:]], 1).astype(BF16)
-    keys_values = jnp.concatenate(xor_blocks(gather_shards(key_value), shard), 0)
+    key_value = after(key_value, dy_routes[1])
+    key_value_y = swap(key_value, 0, 2)
+    query_w = [w_query, query_w_core, query_w_y, swap(query_w_y, 0, 1)]
+    key_value_pair = swap(jnp.concatenate([key_value, key_value_y], 0), 0, 1)
+    keys_values = jnp.concatenate(
+        xor_blocks([key_value, key_value_pair[:rows], key_value_y, key_value_pair[rows:]], shard), 0
+    )
+    out_w_y = swap(after(w_out, query_w_y, key_value), 0, 2)
+    out_w_core = swap(after(w_out, query_w_y), 0, 1)
     cosine_row = jnp.concatenate([cosine, cosine], 1)
     sine_row = jnp.concatenate([-sine, sine], 1)
     seg_query = lax.dynamic_slice_in_dim(segment_ids, shard * rows, rows)[:, None]
     queries, probs, attended = attention_forward(
-        where_shard, h1_rel, query_w, keys_values, cosine_row, sine_row, seg_query, segment_ids[None, :]
-    )
+        where_shard, after(h1_rel, out_w_core, dy_routes[2]), query_w, keys_values, cosine_row, sine_row, seg_query, segment_ids[None, :]
+    )
+    attended_late = after(attended, dy_routes[3])
+    out_w_y = after(out_w_y, attended)
+    out_w = [w_out, out_w_core, out_w_y, swap(out_w_y, 0, 1)]
     mid_state = inputs + sum(
-        dot_nn(attended[:, j * block : (j + 1) * block], out_w[j]) for j in range(4)
+        dot_nn(attended_late[:, j * block : (j + 1) * block], out_w[j]) for j in range(4)
     )
     factor_moe = lax.rsqrt(jnp.mean(mid_state * mid_state, -1, keepdims=True) + EPSILON)
     unit_moe = mid_state * factor_moe
-    small_true = jnp.concatenate(xor_blocks([member[:, 2 * low :] for member in packed], shard), 0)
-    gain_moe = small_true[:, experts + 1].astype(F32)
-    router_pad = jnp.where(jnp.arange(LANES)[None, :] < experts, small_true, 0)
-    router = small_true[:, :experts].astype(F32)
+    small_true = jnp.concatenate(xor_blocks([member[block:, :block] for member in packed], shard), 1)
+    gain_moe = small_true[experts + 1 : experts + 2].astype(F32)
+    router = small_true[:experts].astype(F32)
     h2 = [(unit_moe * gain_moe).astype(BF16)]
 
-    h1_rows = [h1_rel[:, :block]] + [swap(h1_rel[:, j * block : (j + 1) * block], 0, j) for j in (1, 2, 3)]
-    att_rows = [attended[:, :block]] + [
-        swap(attended[:, j * block : (j + 1) * block], 0, j) for j in (1, 2, 3)
-    ]
-
-    for _ in range(3):
-        h2.append(next_plane(h2[-1]))
-    done = [None] * 4
-    add = lambda a, b: (a.astype(F32) + b.astype(F32)).astype(BF16)
-    done[0] = expert_block(where_expert, h2[0], dy_routes[0], router_pad, own, far)
-    message = None
-    mixed = None
-    for j in (1, 2, 3):
-        done[j] = expert_block(where_expert, h2[j], dy_routes[j], router_pad, own, far)
-        message = next_plane(done[j][0] if j == 1 else add(done[j][0], message))
-        mixed = next_plane(done[j][1] if j == 1 else add(done[j][1], mixed))
-    total = done[0][0].astype(F32) + message.astype(F32)
-    layer_out = (mid_state + done[0][1].astype(F32) + mixed.astype(F32)).astype(BF16)
-
+    far_part = after(far_part, attended)
+    far_other = swap(far_part, 0, 1)
     hidden = own[0].shape[1]
     deep = width // 2
-
-    def in_grads(where):
-        return summed_products(
-            where, h2, [[done[j][2] for j in range(4)], [done[j][3] for j in range(4)]], (2,),
-            pl.BlockSpec((rows, deep), lambda i, w: (0, w[0])),
-            pl.BlockSpec((rows, hidden), lambda i, w: (0, i)),
-            pl.BlockSpec((deep, hidden), lambda i, w: (0, i)),
-            (deep, 2 * hidden), "expert_in_grads",
-        )
-
-    def down_grads(where):
-        return summed_products(
-            where, [done[j][4] for j in range(4)], [dy_routes], (2,),
-            pl.BlockSpec((rows, hidden // 2), lambda i, w: (0, 2 * i + w[0])),
-            pl.BlockSpec((rows, width), lambda i, w: (0, 0)),
-            pl.BlockSpec((hidden // 2, width), lambda i, w: (i, 0)),
-            (hidden, width), "expert_down_grads",
-        )
-
-    (down_send,) = down_grads(where_far_core)
-    gate_send, up_send = in_grads(where_far_core)
-    (down_keep,) = down_grads(where_core)
-    gate_keep, up_keep = in_grads(where_core)
-    down_sum = expert_weight_sums(down_send, down_keep, 0, core)
-    gate_sum = expert_weight_sums(gate_send, gate_keep, 1, core)
-    up_sum = expert_weight_sums(up_send, up_keep, 1, core)
-
+    far = (far_part, far_other)
+    where_pair = jnp.stack([expert, core]).astype(jnp.int32)
+
+    mixer_rows = [
+        jnp.concatenate([h1_rel[:, j * block : (j + 1) * block], attended[:, j * block : (j + 1) * block]], 1)
+        for j in range(4)
+    ]
+    mixer_rows = [mixer_rows[0]] + [swap(mixer_rows[j], 0, j) for j in (1, 2, 3)]
+    add = lambda a, b: (a.astype(F32) + b.astype(F32)).astype(BF16)
+    block_of = lambda j, *ready: expert_block(
+        where_pair, after(h2[j], *ready), dy_routes[j], small_true, own, far
+    )
+    h2.append(next_plane(h2[0]))
+    done = [block_of(0)]
+    h2.append(next_plane(after(h2[1], done[0][0])))
+    done.append(block_of(1, done[0][0], *mixer_rows))
+    h2.append(next_plane(after(h2[2], done[1][0])))
+    message = next_plane(done[1][0])
+    done.append(block_of(2, done[1][0]))
+    second = add(done[2][0], message)
+    message = next_plane(second)
+    done.append(block_of(3, second))
+    third = add(done[3][0], message)
+    message = next_plane(third)
+    acts = [done[j][4] for j in range(4)]
+    down_send, down_keep = expert_down_grads(after(where_core, third), acts, dy_routes)
+    in_send, in_keep = expert_in_grads(
+        after(where_core, down_send), h2, [done[j][2] for j in range(4)], [done[j][3] for j in range(4)]
+    )
+    down_swap = swap(down_send, 0, 1)
+    in_swap = swap(in_send, 0, 1)
+    message, down_swap, _ = together(message, down_swap, in_send)
+    down_half = hidden // 2
+    down_far = plus(down_keep[down_half:], down_swap[down_half:])
+    down_received = swap(down_far, 1, 0)
+    message = after(message, down_far)
+    mixed = next_plane(after(done[1][1], message))
+    total = done[0][0].astype(F32) + message.astype(F32)
     named = mask[:, :experts]
-    logits = jnp.where(named, dot_nn(h2[0], router_pad[:, :experts]), MASKED_SCORE)
+    logits = jnp.where(named, dot_nt(h2[0], small_true[:experts]), MASKED_SCORE)
     weights = jnp.where(named, jnp.exp(logits - jnp.max(logits, -1, keepdims=True)), 0.0)
     gate = weights / jnp.sum(weights, -1, keepdims=True)
     gate_grad = total[:, width : width + experts] + total[:, width + experts : width + 2 * experts]
     d_logits = gate * (gate_grad - jnp.sum(gate * gate_grad, -1, keepdims=True))
-    d_h2 = total[:, :width] + jnp.dot(d_logits, router.T, precision=HIGHEST)
+    d_h2 = total[:, :width] + jnp.dot(d_logits, router, precision=HIGHEST)
     router_grad = jnp.dot(d_logits.T, h2[0].astype(F32), precision=HIGHEST)
     d_mid_norm, gain_moe_grad = norm_backward(d_h2, unit_moe, factor_moe, gain_moe)
     d_mid = out_grad.astype(F32) + d_mid_norm
     d_branch = d_mid.astype(BF16)
-    branches = gather_shards(d_branch)
-
-    def mixer_grads(lefts, rights, name):
+    branch_core = swap(d_branch, 0, 1)
+    branch_y = swap(d_branch, 0, 2)
+    branches = [d_branch, branch_core, branch_y, swap(branch_y, 0, 1)]
+
+    def mixer_grads(half, rights, name):
         n = rights[0].shape[1]
         (pieces,) = summed_products(
-            where_expert, lefts, [rights], (1,),
-            pl.BlockSpec((rows, block), lambda i, w: (0, 0)),
+            where_expert, mixer_rows, [rights], (1,),
+            pl.BlockSpec((rows, block), lambda i, w: (0, half)),
             pl.BlockSpec((rows, n), lambda i, w: (0, 0)),
             pl.BlockSpec((N_EXPERT, block // N_EXPERT, n), lambda i, w: (0, 0, 0)),
             (N_EXPERT, block // N_EXPERT, n), name,
         )
-        even, odd = sum_over_planes(pieces)
-        return reorder(where_expert, even, odd)
-
-    out_w_grad = mixer_grads(att_rows, branches, "w_out_grad")
+        return pieces
 
     d_q_pre, d_key_part, d_value_part, d_normed = attention_backward(
         where_shard, d_branch, out_w, attended, queries, probs, keys_values, query_w, cosine_row, sine_row
     )
+    d_q_pre, d_key_part, d_value_part, branch_y, branch_core, in_swap, mixed = together(
+        d_q_pre, d_key_part, d_value_part, branch_y, branch_core, in_swap, mixed
+    )
+    d_q_y = swap(d_q_pre, 0, 2)
+    d_q_core = swap(d_q_pre, 0, 1)
+    branch_far = swap(branch_y, 0, 1)
     d_parts = jnp.concatenate([d_key_part, d_value_part], 1).reshape(N_SHARD, rows, 2 * low)
     d_rel = xor_blocks([d_parts[j] for j in range(4)], shard)
     from_core = swap(jnp.stack([d_rel[1], d_rel[3]]), 0, 1)
+    gate_far = plus(in_keep[0, :, hidden:], in_swap[0, :, hidden:])
+    up_far = plus(in_keep[1, :, hidden:], in_swap[1, :, hidden:])
+    mixed = add(done[2][1], mixed)
+
+    d_q_core, branch_far, from_core, down_received, gate_far, up_far, mixed = together(
+        d_q_core, branch_far, from_core, down_received, gate_far, up_far, mixed
+    )
+    gate_received = swap(gate_far, 1, 0)
+    mixed = next_plane(mixed)
     d_far = add(d_rel[2], from_core[1])
-    d_key_value = d_rel[0].astype(F32) + from_core[0].astype(F32) + swap(d_far, 0, 2).astype(F32)
+    d_far_y = swap(d_far, 0, 2)
+    down_part = plus(down_keep[:down_half].astype(F32) + down_swap[:down_half].astype(F32), down_received)
+    out_pieces = mixer_grads(1, [d_branch, branch_core, branch_y, after(branch_far, down_part)], "w_out_grad")
+
+    d_q_y, out_pieces = together(d_q_y, out_pieces)
+    query_pieces = mixer_grads(0, [d_q_pre, d_q_core, d_q_y, swap(d_q_y, 0, 1)], "w_query_grad")
+
+    query_pieces, d_far_y, mixed = together(query_pieces, d_far_y, mixed)
+    query_sum = PlaneSum(query_pieces, (1, 2, 4))
+    out_sum = PlaneSum(after(out_pieces, query_pieces), (1, 2, 4))
+    down_y = swap(after(down_part, query_pieces), 0, 2)
+    mixed = add(done[3][1], mixed)
+    mixed = next_plane(mixed)
+    d_key_value = d_rel[0].astype(F32) + from_core[0].astype(F32) + d_far_y.astype(F32)
     d_k_pre = rotate(d_key_value[:, :low], cosine, -sine, HEAD)
     d_kv_pre = jnp.concatenate([d_k_pre, d_key_value[:, low:]], 1).astype(BF16)
-    d_pre = gather_shards(jnp.concatenate([d_q_pre, d_kv_pre], 1))
-    in_grad = mixer_grads(h1_rows, d_pre, "w_in_grads")
+
     d_normed = d_normed + jnp.concatenate([dot_nt(d_kv_pre, member) for member in key_value_w], 1)
     d_input_norm, gain_attn_grad = norm_backward(d_normed, unit_rel, factor_attn, gain_rel)
     d_input_norm = jnp.concatenate(
@@ -910,23 +1191,68 @@
 
     rest = jnp.concatenate([gain_moe_grad[None], router_grad, jnp.zeros((6, width), F32)], 0)
     rest = xor_blocks([rest[:, j * block : (j + 1) * block] for j in range(4)], shard)
-    pieces = [
-        jnp.concatenate([gain_attn_grad[None, j * block : (j + 1) * block], rest[j]], 0) for j in range(4)
-    ]
-    from_core = swap(jnp.stack([pieces[1], pieces[3]]), 0, 1)
-    sums = pieces[0] + from_core[0] + swap(pieces[2] + from_core[1], 0, 2)
-    for bit in (1, 2, 4):
-        sums = sums + swap(sums, bit, 0)
+    notes = []
+    for j in range(4):
+        piece = jnp.concatenate([gain_attn_grad[None, j * block : (j + 1) * block], rest[j]], 0)
+        high = piece.astype(BF16)
+        piece = jnp.concatenate([high, (piece - high.astype(F32)).astype(BF16)], 0)
+        notes.append(jnp.concatenate([d_kv_pre, jnp.pad(piece, ((0, 0), (0, 2 * low - block)))], 0))
+    notes_y = swap(jnp.concatenate([notes[2], notes[3]], 0), 0, 2)
+    tall = notes[0].shape[0]
+
+    gate_own = in_keep[0, :, :hidden].astype(F32) + in_swap[0, :, :hidden].astype(F32)
+    gate_part = plus(gate_own, after(gate_received, notes[0]))
+    down_total = plus(down_part, after(down_y, gate_part))
+    up_received = swap(after(up_far, down_total), 1, 0)
+    gate_y = swap(after(gate_part, down_total), 0, 2)
+    layer_out = (mid_state + done[0][1].astype(F32) + after(mixed, down_total).astype(F32)).astype(BF16)
+    token = query_sum.receive(layer_out)
+    token = query_sum.receive(token)
+    notes_y = after(notes_y, token)
+    notes_core = swap(jnp.concatenate([notes[1], notes_y[tall:]], 0), 0, 1)
+    token = out_sum.receive(notes_y)
+    last = key_value_grad(
+        mixer_rows, [notes[0], notes_core[:tall], after(notes_y[:tall], token), notes_core[tall:]], block
+    )
+    last_z = swap(last, 2, 0)
+    down_core = swap(after(down_total, last), 0, 1)
+    token = query_sum.receive(last)
+    token = out_sum.receive(token)
+    down_sum = place_halves(where_core, down_total, after(down_core, token), 0, hidden // 2, width, 0, F32)[None]
+    token = query_sum.receive(down_sum)
+    up_own = in_keep[1, :, :hidden].astype(F32) + in_swap[1, :, :hidden].astype(F32)
+    up_part = plus(up_own, after(up_received, token))
+    up_y = swap(up_part, 0, 2)
+    token = out_sum.receive(up_part)
+    gate_total = plus(gate_part, after(gate_y, token))
+    gate_core = swap(gate_total, 0, 1)
+    last = plus(last, after(last_z, gate_total))
+    token = query_sum.receive(last)
+    token = out_sum.receive(token)
+    last_z = swap(after(last, token), 4, 0)
+    gate_sum = place_halves(where_core, gate_total, after(gate_core, token), 0, deep, hidden, 0, F32)[None]
+    token = out_sum.receive(gate_sum)
+    token = query_sum.receive(token)
+    (query_grad,) = reorder(where_expert, *query_sum.done, (width,), query_sum.order[0])
+    up_total = plus(up_part, after(up_y, token))
+    up_core = swap(up_total, 0, 1)
+    last = plus(last, after(last_z, up_total))
+    last_x = swap(last, 1, 0)
+    up_sum = place_halves(where_core, up_total, after(up_core, last), 0, deep, hidden, 0, F32)[None]
+    token = out_sum.receive(up_sum)
+    (out_w_grad,) = reorder(where_expert, *out_sum.done, (width,), out_sum.order[0])
+    last = last.astype(F32) + after(last_x, token).astype(F32)
+    small_sums = last[block:, :block]
     return (
         layer_out,
         input_grad,
-        sums[0],
-        sums[1],
-        in_grad[:, :width],
-        in_grad[:, width : width + low],
-        in_grad[:, width + low :],
+        small_sums[0],
+        small_sums[1],
+        query_grad,
+        last[:block, :low],
+        last[:block, low:],
         out_w_grad,
-        sums[2 : 2 + experts].T,
+        small_sums[2 : 2 + experts].T,
         gate_sum,
         up_sum,
         down_sum,

time: 635 us -> 464 us (0.73)
  waiting for transfers between devices: 314 us -> 184 us
  local copies, waits for them, and re-layouts: 43.9 us -> 19.2 us
  Pallas kernels: 136 us -> 155 us
  other arithmetic: 59.9 us -> 44.2 us
  starting transfers between devices: 53.5 us -> 39.5 us
    ppermute x61 -> x51, waiting for transfers between devices: 235 us -> 123 us  [swap(): return lax.ppermute(values, AXES, pairs)]
    pallas_call x2 -> x10, Pallas kernels: 11.5 us -> 52.1 us  [the longest x3 14.1 us: place_halves(): pl.pallas_call(place_body, grid_spec=pltpu.PrefetchScalarGridSpec(num_sca...]
    pallas_call x6 -> x2, Pallas kernels: 33.7 us -> 9.28 us  [summed_products(): pl.pallas_call(functools.partial(summed_products_body, parts=parts, sets=...]
    ppermute x12, waiting for transfers between devices: 78.3 us -> 61.2 us  [next_plane(): return lax.ppermute(values, AXES, pairs)]
    ppermute x61 -> x51, starting transfers between devices: 42.6 us -> 32.3 us  [swap(): return lax.ppermute(values, AXES, pairs)]
    convert_element_type x21 -> x26, other arithmetic: 28.1 us -> 19.3 us  [the longest x10 17.5 us: plus(): return (part.astype(F32) + received.astype(F32)).astype(BF16)]
    unnamed x289 -> x175, local copies, waits for them, and re-layouts: 17.5 us -> 11.5 us
  transfers between devices with their start and end apart: 73 -> 63, of which waited for: 33 -> 29; matrix products, arithmetic and copies ran while one was open for 15% -> 13% of each run, Pallas kernels for 21% -> 31%
where the time goes in v2:
time: 464 us; the launch traced here: 455 us
  waiting for transfers between devices  184 us (40%)
  Pallas kernels  155 us (33%)
  other arithmetic  44.2 us (10%)
  starting transfers between devices  39.5 us (9%)
  local copies, waits for them, and re-layouts  19.2 us (4%)
  matrix products  9.65 us (2%)
    ppermute x51, waiting for transfers between devices, swap(): return lax.ppermute(values, AXES, pairs)  123 us
    pallas_call x4, Pallas kernels, expert_block(): pl.pallas_call(expert_body, grid_spec=pltpu.PrefetchScalarGridSpec(num_sc...  62 us
    ppermute x12, waiting for transfers between devices, next_plane(): return lax.ppermute(values, AXES, pairs)  61.2 us
    ppermute x51, starting transfers between devices, swap(): return lax.ppermute(values, AXES, pairs)  32.3 us
    convert_element_type x10, other arithmetic, plus(): return (part.astype(F32) + received.astype(F32)).astype(BF16)  17.5 us
    pallas_call x1, Pallas kernels, attention_backward(): pl.pallas_call(attention_backward_body, grid_spec=pltpu.PrefetchScalarGri...  17.1 us
    pallas_call x1, Pallas kernels, attention_forward(): pl.pallas_call(attention_forward_body, grid_spec=pltpu.PrefetchScalarGrid...  14.9 us
    pallas_call x3, Pallas kernels, place_halves(): pl.pallas_call(place_body, grid_spec=pltpu.PrefetchScalarGridSpec(num_sca...  14.1 us
  transfers between devices with their start and end apart: 63, of which 29 were waited for; matrix products, arithmetic and copies ran while one was open for 13% of the time, Pallas kernels for 31%

profile of v2, /device:TPU:0, one launch (start us, length us, event | category | flops | bytes accessed | tf_op | source)
XLA Modules:
  0.0 454.8 jit_solution(4089421823290162110)
XLA Ops:
  0.7 6.0 %far_halves.1 = bf16[3,768,768]{2,1,0:T(8,128)(2,1)} custom-call(s32[1]{0:T(128)} %bitcast.1.where_ref, bf16[1536,768]{1,0:T(8,128)(2,1)} %bitcast.118, bf16[1536,768]{1,0:T(8,128)(2,1)} %bitcast.127, bf16[768,1536]{1,0:T(8,128)(2,1)} %bitcast.136), custom_call_target="tpu_custom_call" | custom-call | flops 3000000000 | bytes 100000 | tf_op jit(solution)/shard_map/far_halves/pallas_call | solution.py:966
  16.3 7.2 %collective-permute-done = bf16[400,512]{1,0:T(8,128)(2,1)S(1)} collective-permute-done((bf16[400,512]{1,0:T(8,128)(2,1)}, bf16[400,512]{1,0:T(8,128)(2,1)S(1)}, u32[]{:S(2)}, u32[]{:S(2)}) %collective-permute-start) | collective-permute-done | bytes 409632 | tf_op jit(solution)/shard_map/ppermute | solution.py:347
  29.6 7.9 %collective-permute-done.5.dy_ref.refs_9_ = bf16[256,1664]{1,0:T(8,128)(2,1)S(1)} collective-permute-done((bf16[256,1664]{1,0:T(8,128)(2,1)S(1)}, bf16[256,1664]{1,0:T(8,128)(2,1)S(1)}, u32[]{:S(2)}, u32[]{:S(2)}) %collective-permute-start.5) | collective-permute-done | bytes 852000 | tf_op jit(solution)/shard_map/ppermute | solution.py:356
  38.0 15.6 %collective-permute-done.3.w2 = bf16[384,1536]{1,0:T(8,128)(2,1)} collective-permute-done((bf16[384,1536]{1,0:T(8,128)(2,1)}, bf16[384,1536]{1,0:T(8,128)(2,1)}, u32[]{:S(2)}, u32[]{:S(2)}) %collective-permute-start.3) | collective-permute-done | bytes 1179680 | tf_op jit(solution)/shard_map/ppermute | solution.py:347
  54.0 4.6 %collective-permute-done.8 = bf16[256,512]{1,0:T(8,128)(2,1)S(1)} collective-permute-done((bf16[256,512]{1,0:T(8,128)(2,1)}, bf16[256,512]{1,0:T(8,128)(2,1)S(1)}, u32[]{:S(2)}, u32[]{:S(2)}) %collective-permute-start.8) | collective-permute-done | bytes 262176 | tf_op jit(solution)/shard_map/ppermute | solution.py:347
  68.5 14.9 %attention_forward.1 = (bf16[256,1536]{1,0:T(8,128)(2,1)}, bf16[12,256,1024]{2,1,0:T(8,128)(2,1)}, bf16[256,1536]{1,0:T(8,128)(2,1)}) custom-call(s32[1]{0:T(128)} %bitcast.where_ref, bf16[256,1536]{1,0:T(8,128)(2,1)} %copy-done.27, bf16[384,1536]{1,0:T(8,128)(2,1)} %w0.3, bf16[384,1536]{1,0:T(8,128)(2,1)} %collective-permute-done.2.w1, ...), custom_call_target="tpu_custom_call" | custom-call | flops 15000000512 | bytes 100000 | tf_op jit(solution)/shard_map/attention_forward/pallas_call | solution.py:445
  87.4 4.3 collective-permute-done.11.out2
  103.7 15.3 %expert_block.4 = (bf16[256,1664]{1,0:T(8,128)(2,1)S(1)}, bf16[256,1536]{1,0:T(8,128)(2,1)S(1)}, bf16[256,1536]{1,0:T(8,128)(2,1)S(1)}, bf16[256,1536]{1,0:T(8,128)(2,1)S(1)}, bf16[256,1536]{1,0:T(8,128)(2,1)S(1)}) custom-call(s32[2]{0:T(128)S(1)} %pad_add_fusion.where_ref, bf16[256,1536]{1,0:T(8,128)(2,1)S(1)} %multiply_convert_fusion.h2_ref.refs_0_, ...), custom_call_target="tpu_custom_call" | custom-call | flops 20000000000 | bytes 100000 | tf_op jit(solution)/shard_map/expert_block/pallas_call | solution.py:656
  125.2 16.1 %expert_block.5 = (bf16[256,1664]{1,0:T(8,128)(2,1)S(1)}, bf16[256,1536]{1,0:T(8,128)(2,1)}, bf16[256,1536]{1,0:T(8,128)(2,1)S(1)}, bf16[256,1536]{1,0:T(8,128)(2,1)S(1)}, bf16[256,1536]{1,0:T(8,128)(2,1)S(1)}) custom-call(s32[2]{0:T(128)S(1)} %pad_add_fusion.where_ref, bf16[256,1536]{1,0:T(8,128)(2,1)S(1)} %collective-permute-done.15.h2_ref.refs_1_, ...), custom_call_target="tpu_custom_call" | custom-call | flops 20000000000 | bytes 100000 | tf_op jit(solution)/shard_map/expert_block/pallas_call | solution.py:656
  145.2 15.3 %expert_block.6 = (bf16[256,1664]{1,0:T(8,128)(2,1)S(1)}, bf16[256,1536]{1,0:T(8,128)(2,1)S(1)}, bf16[256,1536]{1,0:T(8,128)(2,1)S(1)}, bf16[256,1536]{1,0:T(8,128)(2,1)S(1)}, bf16[256,1536]{1,0:T(8,128)(2,1)S(1)}) custom-call(s32[2]{0:T(128)S(1)} %pad_add_fusion.where_ref, bf16[256,1536]{1,0:T(8,128)(2,1)S(1)} %collective-permute-done.16.h2_ref.refs_2_, ...), custom_call_target="tpu_custom_call" | custom-call | flops 20000000000 | bytes 100000 | tf_op jit(solution)/shard_map/expert_block/pallas_call | solution.py:656
  160.5 4.5 collective-permute-done.21
  165.3 16.6 %collective-permute-done.20.h2_ref.refs_3_ = bf16[256,1536]{1,0:T(8,128)(2,1)S(1)} collective-permute-done((bf16[256,1536]{1,0:T(8,128)(2,1)S(1)}, bf16[256,1536]{1,0:T(8,128)(2,1)S(1)}, u32[]{:S(2)}, u32[]{:S(2)}) %collective-permute-start.20) | collective-permute-done | bytes 786464 | tf_op jit(solution)/shard_map/ppermute | solution.py:356
  181.8 15.3 %expert_block.7 = (bf16[256,1664]{1,0:T(8,128)(2,1)S(1)}, bf16[256,1536]{1,0:T(8,128)(2,1)S(1)}, bf16[256,1536]{1,0:T(8,128)(2,1)S(1)}, bf16[256,1536]{1,0:T(8,128)(2,1)S(1)}, bf16[256,1536]{1,0:T(8,128)(2,1)S(1)}) custom-call(s32[2]{0:T(128)S(1)} %pad_add_fusion.where_ref, bf16[256,1536]{1,0:T(8,128)(2,1)S(1)} %collective-permute-done.20.h2_ref.refs_3_, ...), custom_call_target="tpu_custom_call" | custom-call | flops 20000000000 | bytes 100000 | tf_op jit(solution)/shard_map/expert_block/pallas_call | solution.py:656
  200.3 6.0 %expert_down_grads.1 = (bf16[768,1536]{1,0:T(8,128)(2,1)S(1)}, bf16[768,1536]{1,0:T(8,128)(2,1)S(1)}) custom-call(s32[1]{0:T(128)} %bitcast.1.where_ref, bf16[256,1536]{1,0:T(8,128)(2,1)S(1)} %get-tuple-element.137.refs_0_.refs_4_, bf16[256,1536]{1,0:T(8,128)(2,1)S(1)} %get-tuple-element.138.refs_1_.refs_5_, ...), custom_call_target="tpu_custom_call" | custom-call | flops 20000000000 | bytes 100000 | tf_op jit(solution)/shard_map/expert_down_grads/pallas_call | solution.py:781
  206.6 13.6 %expert_in_grads.1 = (bf16[2,768,1536]{2,1,0:T(8,128)(2,1)}, bf16[2,768,1536]{2,1,0:T(8,128)(2,1)S(1)}) custom-call(s32[1]{0:T(128)} %bitcast.1.where_ref, bf16[256,1536]{1,0:T(8,128)(2,1)S(1)} %multiply_convert_fusion.h2_ref.refs_0_, bf16[256,1536]{1,0:T(8,128)(2,1)S(1)} %collective-permute-done.15.h2_ref.refs_1_, ...), custom_call_target="tpu_custom_call" | custom-call | flops 1000000000 | bytes 100000 | tf_op jit(solution)/shard_map/expert_in_grads/pallas_call | solution.py:751
  221.2 8.3 %collective-permute-done.23 = bf16[256,1664]{1,0:T(8,128)(2,1)S(1)} collective-permute-done((bf16[256,1664]{1,0:T(8,128)(2,1)S(1)}, bf16[256,1664]{1,0:T(8,128)(2,1)S(1)}, u32[]{:S(2)}, u32[]{:S(2)}) %collective-permute-start.23) | collective-permute-done | bytes 852000 | tf_op jit(solution)/shard_map/ppermute | solution.py:356
  236.8 17.1 %attention_backward.1 = (bf16[256,1536]{1,0:T(8,128)(2,1)}, bf16[1024,256]{1,0:T(8,128)(2,1)}, bf16[1024,256]{1,0:T(8,128)(2,1)}, f32[256,1536]{1,0:T(8,128)}) custom-call(s32[1]{0:T(128)} %bitcast.where_ref, bf16[256,1536]{1,0:T(8,128)(2,1)} %fusion.67.branch_ref.refs_4_, bf16[384,1536]{1,0:T(8,128)(2,1)} %out0.1, ...), custom_call_target="tpu_custom_call" | custom-call | flops 16999999488 | bytes 100000 | tf_op jit(solution)/shard_map/attention_backward/pallas_call | solution.py:534
  254.4 4.2 collective-permute-done.28
  270.4 4.7 %w_out_grad.1 = bf16[8,48,1536]{2,1,0:T(8,128)(2,1)} custom-call(s32[1]{0:T(128)} %bitcast.8.where_ref, bf16[256,768]{1,0:T(8,128)(2,1)} %pad_maximum_fusion.10.refs_0_, bf16[256,768]{1,0:T(8,128)(2,1)} %copy-done.83, bf16[256,768]{1,0:T(8,128)(2,1)} %copy-done.84, bf16[256,768]{1,0:T(8,128)(2,1)} %collective-permute-done.19.refs_3_, ...), custom_call_target="tpu_custom_call" | custom-call | flops 5000000000 | bytes 100000 | tf_op jit(solution)/shard_map/w_out_grad/pallas_call | solution.py:709
  275.1 3.9 collective-permute-done.33.refs_6_
  282.7 4.6 %w_query_grad.1 = bf16[8,48,1536]{2,1,0:T(8,128)(2,1)} custom-call(s32[1]{0:T(128)} %bitcast.8.where_ref, bf16[256,768]{1,0:T(8,128)(2,1)} %pad_maximum_fusion.10.refs_0_, bf16[256,768]{1,0:T(8,128)(2,1)} %copy-done.83, bf16[256,768]{1,0:T(8,128)(2,1)} %copy-done.84, bf16[256,768]{1,0:T(8,128)(2,1)} %collective-permute-done.19.refs_3_, ...), custom_call_target="tpu_custom_call" | custom-call | flops 5000000000 | bytes 100000 | tf_op jit(solution)/shard_map/w_query_grad/pallas_call | solution.py:709
  288.7 12.1 %collective-permute-done.36 = bf16[256,1536]{1,0:T(8,128)(2,1)S(1)} collective-permute-done((bf16[256,1536]{1,0:T(8,128)(2,1)S(1)}, bf16[256,1536]{1,0:T(8,128)(2,1)S(1)}, u32[]{:S(2)}, u32[]{:S(2)}) %collective-permute-start.36) | collective-permute-done | bytes 786464 | tf_op jit(solution)/shard_map/ppermute | solution.py:356
  315.2 21.1 %collective-permute-done.38 = bf16[384,1536]{1,0:T(8,128)(2,1)S(1)} collective-permute-done((bf16[384,1536]{1,0:T(8,128)(2,1)S(1)}, bf16[384,1536]{1,0:T(8,128)(2,1)S(1)}, u32[]{:S(2)}, u32[]{:S(2)}) %collective-permute-start.38) | collective-permute-done | bytes 1179680 | tf_op jit(solution)/shard_map/ppermute | solution.py:347
  342.4 4.3 collective-permute-done.42
  358.5 5.9 %collective-permute-done.47 = bf16[2,48,1536]{2,1,0:T(8,128)(2,1)} collective-permute-done((bf16[2,48,1536]{2,1,0:T(8,128)(2,1)}, bf16[2,48,1536]{2,1,0:T(8,128)(2,1)}, u32[]{:S(2)}, u32[]{:S(2)}) %collective-permute-start.47) | collective-permute-done | bytes 294944 | tf_op jit(solution)/shard_map/ppermute | solution.py:347
  366.1 4.7 %place_halves.3 = f32[768,1536]{1,0:T(8,128)} custom-call(s32[1]{0:T(128)} %bitcast.1.where_ref, bf16[384,1536]{1,0:T(8,128)(2,1)} %add_convert_fusion.2.mine_ref, bf16[384,1536]{1,0:T(8,128)(2,1)} %collective-permute-done.52.partner_ref), custom_call_target="tpu_custom_call" | custom-call | flops 3000000000 | bytes 100000 | tf_op jit(solution)/shard_map/place_halves/pallas_call | solution.py:928
  381.3 10.7 %collective-permute-done.45 = bf16[400,512]{1,0:T(8,128)(2,1)S(1)} collective-permute-done((bf16[400,512]{1,0:T(8,128)(2,1)S(1)}, bf16[400,512]{1,0:T(8,128)(2,1)S(1)}, u32[]{:S(2)}, u32[]{:S(2)}) %collective-permute-start.45) | collective-permute-done | bytes 409632 | tf_op jit(solution)/shard_map/ppermute | solution.py:347
  392.1 5.7 %collective-permute-done.54 = bf16[2,48,1536]{2,1,0:T(8,128)(2,1)S(1)} collective-permute-done((bf16[2,48,1536]{2,1,0:T(8,128)(2,1)S(1)}, bf16[2,48,1536]{2,1,0:T(8,128)(2,1)S(1)}, u32[]{:S(2)}, u32[]{:S(2)}) %collective-permute-start.54) | collective-permute-done | bytes 294944 | tf_op jit(solution)/shard_map/ppermute | solution.py:347
  400.4 4.7 %place_halves.4 = f32[1536,768]{1,0:T(8,128)} custom-call(s32[1]{0:T(128)} %bitcast.1.where_ref, bf16[768,768]{1,0:T(8,128)(2,1)} %copy-done.52, bf16[768,768]{1,0:T(8,128)(2,1)} %collective-permute-done.59.partner_ref), custom_call_target="tpu_custom_call" | custom-call | flops 3000000000 | bytes 100000 | tf_op jit(solution)/shard_map/place_halves/pallas_call | solution.py:928
  410.2 3.8 collective-permute-done.57
  417.1 19.8 %collective-permute-done.55 = bf16[400,512]{1,0:T(8,128)(2,1)S(1)} collective-permute-done((bf16[400,512]{1,0:T(8,128)(2,1)S(1)}, bf16[400,512]{1,0:T(8,128)(2,1)S(1)}, u32[]{:S(2)}, u32[]{:S(2)}) %collective-permute-start.55) | collective-permute-done | bytes 409632 | tf_op jit(solution)/shard_map/ppermute | solution.py:347
  441.9 4.7 %place_halves.5 = f32[1536,768]{1,0:T(8,128)} custom-call(s32[1]{0:T(128)} %bitcast.1.where_ref, bf16[768,768]{1,0:T(8,128)(2,1)} %copy-done.53, bf16[768,768]{1,0:T(8,128)(2,1)} %collective-permute-done.62.partner_ref), custom_call_target="tpu_custom_call" | custom-call | flops 3000000000 | bytes 100000 | tf_op jit(solution)/shard_map/place_halves/pallas_call | solution.py:928
  (429 shorter events, 148.6 us)
Async XLA Ops:
  6.7 79.8 %collective-permute-start.13 = (bf16[3,768,768]{2,1,0:T(8,128)(2,1)}, bf16[3,768,768]{2,1,0:T(8,128)(2,1)}, u32[]{:S(2)}, u32[]{:S(2)}) collective-permute-start(bf16[3,768,768]{2,1,0:T(8,128)(2,1)} %far_halves.1), channel_id=1, source_target_pairs={{0,4},{1,5},{2,6},{3,7},{4,0},{5,1},{6,2},{7,3},{8,12},{9,13},{10,... | collective-permute-start | bytes 10616840 | tf_op jit(solution)/shard_map/ppermute | solution.py:347
  14.2 23.3 %collective-permute-start.5 = (bf16[256,1664]{1,0:T(8,128)(2,1)S(1)}, bf16[256,1664]{1,0:T(8,128)(2,1)S(1)}, u32[]{:S(2)}, u32[]{:S(2)}) collective-permute-start(bf16[256,1664]{1,0:T(8,128)(2,1)S(1)} %pad_maximum_fusion.1.dy_ref.refs_8_), channel_id=1, source_target_pairs={{0,8},{1,9},{2,10},{3,11},{4,12},{5,13},{6,14},{7,15},{8,16},{9,17... | collective-permute-start | bytes 2555912 | tf_op jit(solution)/shard_map/ppermute | solution.py:356
  24.4 29.1 %collective-permute-start.3 = (bf16[384,1536]{1,0:T(8,128)(2,1)}, bf16[384,1536]{1,0:T(8,128)(2,1)}, u32[]{:S(2)}, u32[]{:S(2)}) collective-permute-start(bf16[384,1536]{1,0:T(8,128)(2,1)} %w0.3), channel_id=1, source_target_pairs={{0,2},{1,3},{2,0},{3,1},{4,6},{5,7},{6,4},{7,5},{8,10},{9,11},{10,... | collective-permute-start | bytes 3538952 | tf_op jit(solution)/shard_map/ppermute | solution.py:347
  38.0 25.0 %collective-permute-start.6 = (bf16[256,1664]{1,0:T(8,128)(2,1)S(1)}, bf16[256,1664]{1,0:T(8,128)(2,1)S(1)}, u32[]{:S(2)}, u32[]{:S(2)}) collective-permute-start(bf16[256,1664]{1,0:T(8,128)(2,1)S(1)} %collective-permute-done.5.dy_ref.refs_9_), channel_id=1, source_target_pairs={{0,8},{1,9},{2,10},{3,11},{4,12},{5,13},{6,14},{7,15},{8,16},{9,17... | collective-permute-start | bytes 2555912 | tf_op jit(solution)/shard_map/ppermute | solution.py:356
  63.0 28.7 %collective-permute-start.11 = (bf16[384,1536]{1,0:T(8,128)(2,1)}, bf16[384,1536]{1,0:T(8,128)(2,1)}, u32[]{:S(2)}, u32[]{:S(2)}) collective-permute-start(bf16[384,1536]{1,0:T(8,128)(2,1)} %out0.1), channel_id=1, source_target_pairs={{0,2},{1,3},{2,0},{3,1},{4,6},{5,7},{6,4},{7,5},{8,10},{9,11},{10,... | collective-permute-start | bytes 3538952 | tf_op jit(solution)/shard_map/ppermute | solution.py:347
  64.5 27.3 %collective-permute-start.10 = (bf16[256,1664]{1,0:T(8,128)(2,1)S(1)}, bf16[256,1664]{1,0:T(8,128)(2,1)S(1)}, u32[]{:S(2)}, u32[]{:S(2)}) collective-permute-start(bf16[256,1664]{1,0:T(8,128)(2,1)S(1)} %collective-permute-done.6.dy_ref.refs_10_), channel_id=1, source_target_pairs={{0,8},{1,9},{2,10},{3,11},{4,12},{5,13},{6,14},{7,15},{8,16},{9,17... | collective-permute-start | bytes 2555912 | tf_op jit(solution)/shard_map/ppermute | solution.py:356
  91.9 31.8 %collective-permute-start.17 = (bf16[256,768]{1,0:T(8,128)(2,1)S(1)}, bf16[256,768]{1,0:T(8,128)(2,1)S(1)}, u32[]{:S(2)}, u32[]{:S(2)}) collective-permute-start(bf16[256,768]{1,0:T(8,128)(2,1)S(1)} %pad_maximum_fusion.11), channel_id=1, source_target_pairs={{0,1},{1,0},{2,3},{3,2},{4,5},{5,4},{6,7},{7,6},{8,9},{9,8},{10,11... | collective-permute-start | bytes 1179656 | tf_op jit(solution)/shard_map/ppermute | solution.py:347
  92.5 31.2 %collective-permute-start.18 = (bf16[256,768]{1,0:T(8,128)(2,1)S(1)}, bf16[256,768]{1,0:T(8,128)(2,1)S(1)}, u32[]{:S(2)}, u32[]{:S(2)}) collective-permute-start(bf16[256,768]{1,0:T(8,128)(2,1)S(1)} %pad_maximum_fusion.12), channel_id=1, source_target_pairs={{0,2},{1,3},{2,0},{3,1},{4,6},{5,7},{6,4},{7,5},{8,10},{9,11},{10,... | collective-permute-start | bytes 1179656 | tf_op jit(solution)/shard_map/ppermute | solution.py:347
  94.1 31.1 %collective-permute-start.19 = (bf16[256,768]{1,0:T(8,128)(2,1)S(1)}, bf16[256,768]{1,0:T(8,128)(2,1)}, u32[]{:S(2)}, u32[]{:S(2)}) collective-permute-start(bf16[256,768]{1,0:T(8,128)(2,1)S(1)} %pad_maximum_fusion.13), channel_id=1, source_target_pairs={{0,3},{1,2},{2,1},{3,0},{4,7},{5,6},{6,5},{7,4},{8,11},{9,10},{10,... | collective-permute-start | bytes 1179656 | tf_op jit(solution)/shard_map/ppermute | solution.py:347
  101.6 22.1 %collective-permute-start.15 = (bf16[256,1536]{1,0:T(8,128)(2,1)S(1)}, bf16[256,1536]{1,0:T(8,128)(2,1)S(1)}, u32[]{:S(2)}, u32[]{:S(2)}) collective-permute-start(bf16[256,1536]{1,0:T(8,128)(2,1)S(1)} %multiply_convert_fusion.h2_ref.refs_0_), channel_id=1, source_target_pairs={{0,8},{1,9},{2,10},{3,11},{4,12},{5,13},{6,14},{7,15},{8,16},{9,17... | collective-permute-start | bytes 2359304 | tf_op jit(solution)/shard_map/ppermute | solution.py:356
  141.3 23.6 %collective-permute-start.21 = (bf16[256,1664]{1,0:T(8,128)(2,1)S(1)}, bf16[256,1664]{1,0:T(8,128)(2,1)S(1)}, u32[]{:S(2)}, u32[]{:S(2)}) collective-permute-start(bf16[256,1664]{1,0:T(8,128)(2,1)S(1)} %get-tuple-element.130), channel_id=1, source_target_pairs={{0,8},{1,9},{2,10},{3,11},{4,12},{5,13},{6,14},{7,15},{8,16},{9,17... | collective-permute-start | bytes 2555912 | tf_op jit(solution)/shard_map/ppermute | solution.py:356
  144.8 37.0 %collective-permute-start.20 = (bf16[256,1536]{1,0:T(8,128)(2,1)S(1)}, bf16[256,1536]{1,0:T(8,128)(2,1)S(1)}, u32[]{:S(2)}, u32[]{:S(2)}) collective-permute-start(bf16[256,1536]{1,0:T(8,128)(2,1)S(1)} %collective-permute-done.16.h2_ref.refs_2_), channel_id=1, source_target_pairs={{0,8},{1,9},{2,10},{3,11},{4,12},{5,13},{6,14},{7,15},{8,16},{9,17... | collective-permute-start | bytes 2359304 | tf_op jit(solution)/shard_map/ppermute | solution.py:356
  165.2 33.7 %collective-permute-start.22 = (bf16[256,1664]{1,0:T(8,128)(2,1)S(1)}, bf16[256,1664]{1,0:T(8,128)(2,1)S(1)}, u32[]{:S(2)}, u32[]{:S(2)}) collective-permute-start(bf16[256,1664]{1,0:T(8,128)(2,1)S(1)} %add_convert_fusion.8), channel_id=1, source_target_pairs={{0,8},{1,9},{2,10},{3,11},{4,12},{5,13},{6,14},{7,15},{8,16},{9,17... | collective-permute-start | bytes 2555912 | tf_op jit(solution)/shard_map/ppermute | solution.py:356
  206.3 23.2 %collective-permute-start.24 = (bf16[768,1536]{1,0:T(8,128)(2,1)S(1)}, bf16[768,1536]{1,0:T(8,128)(2,1)S(1)}, u32[]{:S(2)}, u32[]{:S(2)}) collective-permute-start(bf16[768,1536]{1,0:T(8,128)(2,1)S(1)} %get-tuple-element.141), channel_id=1, source_target_pairs={{0,1},{1,0},{2,3},{3,2},{4,5},{5,4},{6,7},{7,6},{8,9},{9,8},{10,11... | collective-permute-start | bytes 7077896 | tf_op jit(solution)/shard_map/ppermute | solution.py:347
  206.4 23.1 %collective-permute-start.23 = (bf16[256,1664]{1,0:T(8,128)(2,1)S(1)}, bf16[256,1664]{1,0:T(8,128)(2,1)S(1)}, u32[]{:S(2)}, u32[]{:S(2)}) collective-permute-start(bf16[256,1664]{1,0:T(8,128)(2,1)S(1)} %add_convert_fusion.7), channel_id=1, source_target_pairs={{0,8},{1,9},{2,10},{3,11},{4,12},{5,13},{6,14},{7,15},{8,16},{9,17... | collective-permute-start | bytes 2555912 | tf_op jit(solution)/shard_map/ppermute | solution.py:356
  220.2 38.4 %collective-permute-start.27 = (bf16[2,768,1536]{2,1,0:T(8,128)(2,1)}, bf16[2,768,1536]{2,1,0:T(8,128)(2,1)}, u32[]{:S(2)}, u32[]{:S(2)}) collective-permute-start(bf16[2,768,1536]{2,1,0:T(8,128)(2,1)} %get-tuple-element.151), channel_id=1, source_target_pairs={{0,1},{1,0},{2,3},{3,2},{4,5},{5,4},{6,7},{7,6},{8,9},{9,8},{10,11... | collective-permute-start | bytes 14155784 | tf_op jit(solution)/shard_map/ppermute | solution.py:347
  234.5 24.2 %collective-permute-start.25 = (bf16[256,1536]{1,0:T(8,128)(2,1)}, bf16[256,1536]{1,0:T(8,128)(2,1)}, u32[]{:S(2)}, u32[]{:S(2)}) collective-permute-start(bf16[256,1536]{1,0:T(8,128)(2,1)} %fusion.67.branch_ref.refs_4_), channel_id=1, source_target_pairs={{0,2},{1,3},{2,0},{3,1},{4,6},{5,7},{6,4},{7,5},{8,10},{9,11},{10,... | collective-permute-start | bytes 2359304 | tf_op jit(solution)/shard_map/ppermute | solution.py:347
  236.1 22.5 %collective-permute-start.26 = (bf16[256,1536]{1,0:T(8,128)(2,1)}, bf16[256,1536]{1,0:T(8,128)(2,1)}, u32[]{:S(2)}, u32[]{:S(2)}) collective-permute-start(bf16[256,1536]{1,0:T(8,128)(2,1)} %fusion.67.branch_ref.refs_4_), channel_id=1, source_target_pairs={{0,1},{1,0},{2,3},{3,2},{4,5},{5,4},{6,7},{7,6},{8,9},{9,8},{10,11... | collective-permute-start | bytes 2359304 | tf_op jit(solution)/shard_map/ppermute | solution.py:347
  236.1 30.2 %collective-permute-start.32 = (bf16[384,1536]{1,0:T(8,128)(2,1)}, bf16[384,1536]{1,0:T(8,128)(2,1)}, u32[]{:S(2)}, u32[]{:S(2)}) collective-permute-start(bf16[384,1536]{1,0:T(8,128)(2,1)} %add_convert_fusion.6), channel_id=1, source_target_pairs={{0,4},{1,5},{2,6},{3,7},{4,0},{5,1},{6,2},{7,3},{8,12},{9,13},{10,... | collective-permute-start | bytes 3538952 | tf_op jit(solution)/shard_map/ppermute | solution.py:347
  236.7 21.9 %collective-permute-start.28 = (bf16[256,1536]{1,0:T(8,128)(2,1)}, bf16[256,1536]{1,0:T(8,128)(2,1)}, u32[]{:S(2)}, u32[]{:S(2)}) collective-permute-start(bf16[256,1536]{1,0:T(8,128)(2,1)} %get-tuple-element.162), channel_id=1, source_target_pairs={{0,8},{1,9},{2,10},{3,11},{4,12},{5,13},{6,14},{7,15},{8,16},{9,17... | collective-permute-start | bytes 2359304 | tf_op jit(solution)/shard_map/ppermute | solution.py:356
  280.3 30.5 %collective-permute-start.39 = (bf16[768,768]{1,0:T(8,128)(2,1)S(1)}, bf16[768,768]{1,0:T(8,128)(2,1)}, u32[]{:S(2)}, u32[]{:S(2)}) collective-permute-start(bf16[768,768]{1,0:T(8,128)(2,1)S(1)} %copy-done.51), channel_id=1, source_target_pairs={{0,4},{1,5},{2,6},{3,7},{4,0},{5,1},{6,2},{7,3},{8,12},{9,13},{10,... | collective-permute-start | bytes 3538952 | tf_op jit(solution)/shard_map/ppermute | solution.py:347
  305.8 43.9 %collective-permute-start.44 = (bf16[2,2,48,1536]{3,2,0,1:T(8,128)(2,1)S(1)}, bf16[2,2,48,1536]{3,2,0,1:T(8,128)(2,1)S(1)}, u32[]{:S(2)}, u32[]{:S(2)}) collective-permute-start(bf16[2,2,48,1536]{3,2,0,1:T(8,128)(2,1)S(1)} %bitcast.156), channel_id=1, source_target_pairs={{0,4},{1,5},{2,6},{3,7},{4,0},{5,1},{6,2},{7,3},{8,12},{9,13},{10,... | collective-permute-start | bytes 1769480 | tf_op jit(solution)/shard_map/ppermute | solution.py:347
  307.4 28.9 %collective-permute-start.38 = (bf16[384,1536]{1,0:T(8,128)(2,1)S(1)}, bf16[384,1536]{1,0:T(8,128)(2,1)S(1)}, u32[]{:S(2)}, u32[]{:S(2)}) collective-permute-start(bf16[384,1536]{1,0:T(8,128)(2,1)S(1)} %copy-done.40), channel_id=1, source_target_pairs={{0,2},{1,3},{2,0},{3,1},{4,6},{5,7},{6,4},{7,5},{8,10},{9,11},{10,... | collective-permute-start | bytes 3538952 | tf_op jit(solution)/shard_map/ppermute | solution.py:347
  307.9 29.7 %collective-permute-start.37 = (bf16[256,1536]{1,0:T(8,128)(2,1)S(1)}, bf16[256,1536]{1,0:T(8,128)(2,1)S(1)}, u32[]{:S(2)}, u32[]{:S(2)}) collective-permute-start(bf16[256,1536]{1,0:T(8,128)(2,1)S(1)} %add_convert_fusion.10), channel_id=1, source_target_pairs={{0,8},{1,9},{2,10},{3,11},{4,12},{5,13},{6,14},{7,15},{8,16},{9,17... | collective-permute-start | bytes 2359304 | tf_op jit(solution)/shard_map/ppermute | solution.py:356
  308.4 31.4 %collective-permute-start.41 = (bf16[2,2,48,1536]{3,2,0,1:T(8,128)(2,1)S(1)}, bf16[2,2,48,1536]{3,2,0,1:T(8,128)(2,1)S(1)}, u32[]{:S(2)}, u32[]{:S(2)}) collective-permute-start(bf16[2,2,48,1536]{3,2,0,1:T(8,128)(2,1)S(1)} %bitcast.157), channel_id=1, source_target_pairs={{0,4},{1,5},{2,6},{3,7},{4,0},{5,1},{6,2},{7,3},{8,12},{9,13},{10,... | collective-permute-start | bytes 1769480 | tf_op jit(solution)/shard_map/ppermute | solution.py:347
  310.8 38.1 %collective-permute-start.40 = (bf16[576,512]{1,0:T(8,128)(2,1)S(1)}, bf16[576,512]{1,0:T(8,128)(2,1)S(1)}, u32[]{:S(2)}, u32[]{:S(2)}) collective-permute-start(bf16[576,512]{1,0:T(8,128)(2,1)S(1)} %pad_maximum_fusion.3), channel_id=1, source_target_pairs={{0,2},{1,3},{2,0},{3,1},{4,6},{5,7},{6,4},{7,5},{8,10},{9,11},{10,... | collective-permute-start | bytes 1769480 | tf_op jit(solution)/shard_map/ppermute | solution.py:347
  341.0 30.7 %collective-permute-start.50 = (bf16[768,768]{1,0:T(8,128)(2,1)S(1)}, bf16[768,768]{1,0:T(8,128)(2,1)}, u32[]{:S(2)}, u32[]{:S(2)}) collective-permute-start(bf16[768,768]{1,0:T(8,128)(2,1)S(1)} %copy-done.50), channel_id=1, source_target_pairs={{0,4},{1,5},{2,6},{3,7},{4,0},{5,1},{6,2},{7,3},{8,12},{9,13},{10,... | collective-permute-start | bytes 3538952 | tf_op jit(solution)/shard_map/ppermute | solution.py:347
  342.0 32.7 %collective-permute-start.46 = (bf16[768,768]{1,0:T(8,128)(2,1)S(1)}, bf16[768,768]{1,0:T(8,128)(2,1)}, u32[]{:S(2)}, u32[]{:S(2)}) collective-permute-start(bf16[768,768]{1,0:T(8,128)(2,1)S(1)} %fusion.3), channel_id=1, source_target_pairs={{0,2},{1,3},{2,0},{3,1},{4,6},{5,7},{6,4},{7,5},{8,10},{9,11},{10,... | collective-permute-start | bytes 3538952 | tf_op jit(solution)/shard_map/ppermute | solution.py:347
  376.4 24.0 %collective-permute-start.59 = (bf16[768,768]{1,0:T(8,128)(2,1)S(1)}, bf16[768,768]{1,0:T(8,128)(2,1)}, u32[]{:S(2)}, u32[]{:S(2)}) collective-permute-start(bf16[768,768]{1,0:T(8,128)(2,1)S(1)} %add_convert_fusion.1.mine_ref), channel_id=1, source_target_pairs={{0,1},{1,0},{2,3},{3,2},{4,5},{5,4},{6,7},{7,6},{8,9},{9,8},{10,11... | collective-permute-start | bytes 3538952 | tf_op jit(solution)/shard_map/ppermute | solution.py:347
  381.0 33.0 %collective-permute-start.56 = (bf16[768,768]{1,0:T(8,128)(2,1)S(1)}, bf16[768,768]{1,0:T(8,128)(2,1)}, u32[]{:S(2)}, u32[]{:S(2)}) collective-permute-start(bf16[768,768]{1,0:T(8,128)(2,1)S(1)} %fusion.2), channel_id=1, source_target_pairs={{0,2},{1,3},{2,0},{3,1},{4,6},{5,7},{6,4},{7,5},{8,10},{9,11},{10,... | collective-permute-start | bytes 3538952 | tf_op jit(solution)/shard_map/ppermute | solution.py:347
  415.6 26.3 %collective-permute-start.62 = (bf16[768,768]{1,0:T(8,128)(2,1)S(1)}, bf16[768,768]{1,0:T(8,128)(2,1)}, u32[]{:S(2)}, u32[]{:S(2)}) collective-permute-start(bf16[768,768]{1,0:T(8,128)(2,1)S(1)} %add_convert_fusion.mine_ref), channel_id=1, source_target_pairs={{0,1},{1,0},{2,3},{3,2},{4,5},{5,4},{6,7},{7,6},{8,9},{9,8},{10,11... | collective-permute-start | bytes 3538952 | tf_op jit(solution)/shard_map/ppermute | solution.py:347
  416.1 30.5 %collective-permute-start.61 = (bf16[2,2,48,1536]{3,2,1,0:T(8,128)(2,1)}, bf16[2,2,48,1536]{3,2,1,0:T(8,128)(2,1)S(1)}, u32[]{:S(2)}, u32[]{:S(2)}) collective-permute-start(bf16[2,2,48,1536]{3,2,1,0:T(8,128)(2,1)} %pad_maximum_fusion.7), channel_id=1, source_target_pairs={{0,4},{1,5},{2,6},{3,7},{4,0},{5,1},{6,2},{7,3},{8,12},{9,13},{10,... | collective-permute-start | bytes 1769480 | tf_op jit(solution)/shard_map/ppermute | solution.py:347
  (116 other events, 1364.0 us)
